TPU v7x, 32 devices: a whole 2x2x4 slice. The times are simulated.
32 devices in a mesh: dp: 16 (over z, y, core), blk: 2 (over x).
Axes of the slice: x: 2, y: 2, z: 4, core: 2. Of those that a mesh axis runs over, the one named last changes fastest.
Arguments:
- resid: bfloat16 [512, 2048], P('dp'), may hold values from -40 to 40
- queries: bfloat16 [512, 16, 128], P('dp', 'blk'), may hold values from -60 to 60
- new_kv: bfloat16 [512, 2, 8, 128], P('dp', None, 'blk'), may hold values from -6 to 6
- prefix_pool: bfloat16 [512, 128, 2, 8, 128], P('dp', None, None, 'blk'), may hold values from -6 to 6
- page_table: int32 [16, 32], P('dp'), may hold values from 0 to 31, each once within a row
- prompt_len: int32 [16], P('dp'), may hold values from 1 to 4096, 32768 in all
- tail_pool: bfloat16 [256, 128, 2, 8, 128], P('dp', None, None, 'blk'), may hold values from -6 to 6
- tail_len: int32 [16, 16], P('dp'), may hold values from 1 to 128, 1024 in all within a row
- migration: int32 [256], replicated, may hold values from 0 to 255, each once
- out_w: bfloat16 [2048, 2048], P('blk'), may hold values from -0.125 to 0.125
- mlp_gain: bfloat16 [2048], replicated, may hold values from 0.099609375 to 1.8984375
- gate_w: bfloat16 [2048, 6144], P('blk', 'dp'), may hold values from -0.125 to 0.125
- up_w: bfloat16 [2048, 6144], P('blk', 'dp'), may hold values from -0.125 to 0.125
- down_w: bfloat16 [6144, 2048], P('dp', 'blk'), may hold values from -0.078125 to 0.078125
- final_gain: bfloat16 [2048], P('blk'), may hold values from 0.099609375 to 1.8984375
- score_w: bfloat16 [2048], P('blk'), may hold values from -0.125 to 0.125
Outputs:
- hidden_out: bfloat16 [512, 2048], P('dp', 'blk')
- score: float32 [512], P('dp')
Inputs may be any that keep to these rules, and one draw needn't show every extreme that they name: `page_table`: each row lists every page of the device's pool once. `migration`: names every continuation once.
All inputs are finite; a program needn't handle non-finite values. No bound on the sum of `prompt_len` on one device may be relied on, other than what follows from the above.
Results may differ from a plain program's by a relative error of at most 0.012.
Values may be sent and summed in bfloat16 or wider, within the bound.
No kernel may reach another device: no remote copies, remote signals or barrier semaphores. Data moves between devices by JAX's collectives and lax.ppermute only.
A program may use at most 64 MiB of HBM per device.

v0:
```python
import functools
import math

import jax
import jax.numpy as jnp
from jax import lax
from jax.experimental import pallas as pl
from jax.experimental.pallas import tpu as pltpu
from jax.sharding import Mesh
from jax.sharding import PartitionSpec as P

D = 2048
NEW = 2
NEG = -1e30
EPS = 1e-06
MIB = 1 << 20
ATTENTION_VMEM = 60 * MIB
UNITS_VMEM = 6 * MIB
DOWN_VMEM = 12 * MIB

VMEM = pl.BlockSpec(memory_space=pltpu.VMEM)
SMEM = pl.BlockSpec(memory_space=pltpu.SMEM)
ANY = pl.BlockSpec(memory_space=pl.ANY)


def mm(a, b):
    return jnp.dot(a, b, preferred_element_type=jnp.float32)


def mm_t(a, b):
    return lax.dot_general(a, b, (((1,), (1,)), ((), ())), preferred_element_type=jnp.float32)


def attention_kernel(
    dims,
    table,
    prompt_len,
    tail_len,
    queries,
    new_kv,
    pool,
    tails,
    out_w,
    own_ref,
    send_ref,
    pages,
    tail_buf,
    w_buf,
    q_buf,
    new_buf,
    keys_apart,
    apart,
    tail_keys,
    tail_apart,
    q_wide,
    q_rows,
    q_pairs,
    new_wide,
    fresh_scores,
    tail_scores,
    scores,
    top,
    total,
    acc,
    attn,
    page_sems,
    tail_sems,
    sems,
):
    rows, heads, groups, width, n_pages, page, conts, tail, pair = dims
    repeat = heads // groups
    step = 2 * groups
    pairs = groups // pair
    stack = repeat * rows
    page_rows = page * step
    chunk_pages = math.gcd(16, n_pages)
    chunk = chunk_pages * page
    chunk_rows = chunk * step
    quad = 8 // NEW
    quads = conts // quad
    quad_keys = quad * tail
    quad_rows = quad_keys * step
    factor = math.log2(math.e) / math.sqrt(width)
    length = prompt_len[0]
    chunks = (length + chunk - 1) // chunk

    def page_copy(logical):
        physical = table[0, logical]
        return pltpu.make_async_copy(
            pool.at[pl.ds(pl.multiple_of(physical * page_rows, page_rows), page_rows), :],
            pages.at[pl.ds(pl.multiple_of(logical * page_rows, page_rows), page_rows), :],
            page_sems.at[logical],
        )

    def tail_copy(index):
        return pltpu.make_async_copy(
            tails.at[pl.ds(index * quad_rows, quad_rows), :],
            tail_buf.at[pl.ds(index * quad_rows, quad_rows), :],
            tail_sems.at[index],
        )

    q_copy = pltpu.make_async_copy(queries, q_buf, sems.at[0])
    new_copy = pltpu.make_async_copy(new_kv, new_buf, sems.at[1])
    w_copy = pltpu.make_async_copy(out_w, w_buf, sems.at[2])
    q_copy.start()
    new_copy.start()
    for index in range(quads):
        tail_copy(index).start()

    @pl.loop(0, chunks * chunk_pages)
    def _(logical):
        page_copy(logical).start()

    w_copy.start()

    block = 256
    tokens = block // step
    to = lax.broadcasted_iota(jnp.int32, (block, block), 0)
    came = lax.broadcasted_iota(jnp.int32, (block, block), 1)
    sort = (came == (to % tokens) * step + to // tokens).astype(jnp.bfloat16)

    def take_apart(buf, start, count, outs, places):
        for two in range(count // (2 * block)):
            x0 = buf[pl.ds(start + two * 2 * block, block), :]
            x1 = buf[pl.ds(start + (two * 2 + 1) * block, block), :]
            y = mm(sort, jnp.concatenate([x0, x1], axis=1)).astype(jnp.bfloat16)
            for side in range(2):
                for j in range(step):
                    kind, g = j // groups, j % groups
                    t = pl.ds(places[kind] + (2 * two + side) * tokens, tokens)
                    lane = (g % pair) * width
                    outs[kind][g // pair, t, lane : lane + width] = y[
                        j * tokens : (j + 1) * tokens, side * width : (side + 1) * width
                    ]

    def blocks(x):
        return [x[:, i * 128 : (i + 1) * 128] for i in range(x.shape[1] // 128)]

    q_copy.wait()
    new_copy.wait()
    q_wide[...] = q_buf[...].astype(jnp.float32)
    new_wide[...] = new_buf[...].astype(jnp.float32)
    if pair > 1:
        q_rows[...] = jnp.zeros_like(q_rows)
    for g in range(groups):
        for r in range(repeat):
            at = (g % pair) * stack + r * rows
            lane = (g % pair) * width
            q_rows[g // pair, at : at + rows, lane : lane + width] = q_wide[
                pl.ds(g * repeat + r, rows, stride=heads), :
            ]

    q_pairs[...] = q_rows[...].astype(jnp.bfloat16)

    def fresh(first, n):
        parts = [
            new_wide[pl.ds(first + n * pair + i, rows, stride=step), :] for i in range(pair)
        ]
        return jnp.concatenate(parts, axis=1).astype(jnp.bfloat16)

    row = lax.broadcasted_iota(jnp.int32, (rows, rows), 0)
    key = lax.broadcasted_iota(jnp.int32, (rows, rows), 1)
    fresh_ok = (row // NEW == key // NEW) & (key <= row)
    fresh_ok = jnp.concatenate([fresh_ok] * (pair * repeat), axis=0)
    for n in range(pairs):
        s = jnp.where(fresh_ok, mm_t(q_pairs[n], fresh(0, n)) * factor, NEG)
        fresh_scores[n] = s
        top[n] = jnp.broadcast_to(jnp.max(s, axis=1, keepdims=True), top.shape[1:])

    def quad_places(index):
        starts = [i * rows + index * 8 for i in range(pair * repeat)]
        return [slice(at, at + 8) for at in starts]

    quad_row = lax.broadcasted_iota(jnp.int32, (8, quad_keys), 0)
    quad_key = lax.broadcasted_iota(jnp.int32, (8, quad_keys), 1)
    for index in range(quads):
        tail_copy(index).wait()
    for index in range(quads):
        outs, at = (tail_keys, tail_apart), index * quad_keys
        take_apart(tail_buf, index * quad_rows, quad_rows, outs, (at, at))
        reach = jnp.zeros((8, quad_keys), jnp.int32)
        for c in range(quad):
            reach = jnp.where(
                quad_key // tail == c, tail_len[0, index * quad + c] + c * tail, reach
            )
        ok = (quad_row // NEW == quad_key // tail) & (quad_key < reach)
        ok = jnp.concatenate([ok] * (pair * repeat), axis=0)
        keys = slice(index * quad_keys, (index + 1) * quad_keys)
        for n in range(pairs):
            q = jnp.concatenate([q_rows[n, a, :] for a in quad_places(index)], axis=0)
            s = mm_t(q.astype(jnp.bfloat16), tail_keys[n, keys, :]) * factor
            s = jnp.where(ok, s, NEG)
            tail_scores[n, index] = s
            high = functools.reduce(jnp.maximum, blocks(s))
            for i, a in enumerate(quad_places(index)):
                top[n, a, :] = jnp.maximum(top[n, a, :], high[i * 8 : (i + 1) * 8])

    part = min(256, chunk)
    place = lax.broadcasted_iota(jnp.int32, (8, part), 1)

    @pl.loop(0, chunks)
    def _(index):
        for i in range(chunk_pages):
            page_copy(index * chunk_pages + i).wait()
        first = pl.multiple_of(index * chunk, chunk)
        row = pl.multiple_of(index * chunk_rows, chunk_rows)
        for at in range(0, chunk, part):
            outs, places = (keys_apart, apart), (at, first + at)
            take_apart(pages, row + at * step, part * step, outs, places)
            ok = place[0:1] < length - (index * chunk + at)
            for n in range(pairs):
                s = mm_t(q_pairs[n], keys_apart[n, at : at + part, :]) * factor
                s = jnp.where(ok, s, NEG)
                scores[n, :, pl.ds(first + at, part)] = s
                top[n] = functools.reduce(jnp.maximum, blocks(s), top[n])

    for n in range(pairs):
        high = jnp.broadcast_to(jnp.max(top[n], axis=1, keepdims=True), top.shape[1:])
        top[n] = high
        p = jnp.exp2(fresh_scores[n] - high[:, :rows])
        lane = lax.broadcasted_iota(jnp.int32, total.shape[1:], 1)
        total[n] = jnp.where(lane == 0, jnp.sum(p, axis=1, keepdims=True), 0.0)
        acc[n] = mm(p.astype(jnp.bfloat16), fresh(groups, n))

    def weigh(s, high):
        parts = [jnp.exp2(part - high) for part in blocks(s)]
        return jnp.concatenate(parts, axis=1).astype(jnp.bfloat16), functools.reduce(jnp.add, parts)

    for index in range(quads):
        keys = slice(index * quad_keys, (index + 1) * quad_keys)
        for n in range(pairs):
            high = jnp.concatenate([top[n, a, :] for a in quad_places(index)], axis=0)
            p, added = weigh(tail_scores[n, index], high)
            value = mm(p, tail_apart[n, keys, :])
            for i, a in enumerate(quad_places(index)):
                total[n, a, :] = total[n, a, :] + added[i * 8 : (i + 1) * 8]
                acc[n, a, :] = acc[n, a, :] + value[i * 8 : (i + 1) * 8]

    @pl.loop(0, chunks)
    def _(index):
        first = pl.multiple_of(index * chunk, chunk)
        for n in range(pairs):
            p, added = weigh(scores[n, :, pl.ds(first, chunk)], top[n])
            total[n] = total[n] + added
            acc[n] = acc[n] + mm(p, apart[n, pl.ds(first, chunk), :])

    for g in range(groups):
        at, lane = (g % pair) * stack, (g % pair) * width
        out = acc[g // pair, at : at + stack, lane : lane + width]
        out = out / jnp.sum(total[g // pair, at : at + stack, :], axis=1, keepdims=True)
        out = out.astype(jnp.bfloat16)
        for r in range(repeat):
            head = g * repeat + r
            attn[:, head * width : (head + 1) * width] = out[r * rows : (r + 1) * rows]
    w_copy.wait()
    value = mm(attn[...], w_buf[...])
    own_ref[...] = value
    send_ref[...] = value.astype(jnp.bfloat16)


def attention(queries, new_kv, pool, table, prompt_len, tails, tail_len, out_w):
    rows, heads, width = queries.shape
    n_pages, page, _, groups, _ = pool.shape
    conts, tail = tails.shape[:2]
    step = 2 * groups
    features = out_w.shape[1]
    quads = conts * NEW // 8
    pair = 2 if groups % 2 == 0 else 1
    pairs = groups // pair
    repeat = heads // groups
    stack = pair * repeat * rows
    return pl.pallas_call(
        functools.partial(
            attention_kernel, (rows, heads, groups, width, n_pages, page, conts, tail, pair)
        ),
        out_shape=(
            jax.ShapeDtypeStruct((rows, features), jnp.float32),
            jax.ShapeDtypeStruct((rows, features), jnp.bfloat16),
        ),
        in_specs=[SMEM, SMEM, SMEM, ANY, ANY, ANY, ANY, ANY],
        out_specs=(VMEM, VMEM),
        scratch_shapes=[
            pltpu.VMEM((n_pages * page * step, width), jnp.bfloat16),
            pltpu.VMEM((conts * tail * step, width), jnp.bfloat16),
            pltpu.VMEM(out_w.shape, jnp.bfloat16),
            pltpu.VMEM((rows * heads, width), jnp.bfloat16),
            pltpu.VMEM((rows * step, width), jnp.bfloat16),
            pltpu.VMEM((pairs, n_pages * page, pair * width), jnp.bfloat16),
            pltpu.VMEM((pairs, n_pages * page, pair * width), jnp.bfloat16),
            pltpu.VMEM((pairs, conts * tail, pair * width), jnp.bfloat16),
            pltpu.VMEM((pairs, conts * tail, pair * width), jnp.bfloat16),
            pltpu.VMEM((rows * heads, width), jnp.float32),
            pltpu.VMEM((pairs, stack, pair * width), jnp.float32),
            pltpu.VMEM((pairs, stack, pair * width), jnp.bfloat16),
            pltpu.VMEM((rows * step, width), jnp.float32),
            pltpu.VMEM((pairs, stack, rows), jnp.float32),
            pltpu.VMEM((pairs, quads, pair * repeat * 8, 8 // NEW * tail), jnp.float32),
            pltpu.VMEM((pairs, stack, n_pages * page), jnp.float32),
            pltpu.VMEM((pairs, stack, 128), jnp.float32),
            pltpu.VMEM((pairs, stack, 128), jnp.float32),
            pltpu.VMEM((pairs, stack, pair * width), jnp.float32),
            pltpu.VMEM((rows, heads * width), jnp.bfloat16),
            pltpu.SemaphoreType.DMA((n_pages,)),
            pltpu.SemaphoreType.DMA((quads,)),
            pltpu.SemaphoreType.DMA((3,)),
        ],
        compiler_params=pltpu.CompilerParams(vmem_limit_bytes=ATTENTION_VMEM),
        name="attention",
    )(
        table,
        prompt_len,
        tail_len,
        queries.reshape(rows * heads, width),
        new_kv.reshape(rows * step, width),
        pool.reshape(n_pages * page * step, width),
        tails.reshape(conts * tail * step, width),
        out_w,
    )


def norm_kernel(n, block, own, other, gain, *refs):
    normed, middle, whole = refs[n:]
    copies, rows, features = normed.shape
    mid = own[...] + other[...].astype(jnp.float32)
    scale = lax.rsqrt(jnp.mean(mid * mid, axis=1, keepdims=True) + EPS)
    whole[...] = mid
    start = pl.multiple_of(block[0] * features, features)
    part = whole[:, pl.ds(start, features)]
    out = (part * scale * gain[:, pl.ds(start, features)]).astype(jnp.bfloat16)
    for index in range(copies):
        normed[index] = out
    middle[...] = part


def normalize(block, own, other, gain, features, copies, ahead):
    rows = own.shape[0]
    return pl.pallas_call(
        functools.partial(norm_kernel, len(ahead)),
        out_shape=(
            jax.ShapeDtypeStruct((copies, rows, features), jnp.bfloat16),
            jax.ShapeDtypeStruct((rows, features), jnp.float32),
        ),
        in_specs=[SMEM, VMEM, VMEM, VMEM] + [ANY] * len(ahead),
        out_specs=(VMEM, VMEM),
        scratch_shapes=[pltpu.VMEM(own.shape, jnp.float32)],
        compiler_params=pltpu.CompilerParams(vmem_limit_bytes=4 * MIB),
        name="normalize",
    )(block, own, other, gain.astype(jnp.float32).reshape(1, -1), *ahead)


def units_kernel(n, block, *refs):
    pieces, gate_w, up_w, outs, held, sums = refs[:n], *refs[n : n + 2], refs[n + 2 : -2], *refs[-2:]
    at = 0
    for piece in pieces:
        held[at : at + piece.shape[0], :] = piece[...]
        at += piece.shape[0]
    units = gate_w.shape[1]
    sums[:, :units] = mm(held[...], gate_w[...])
    sums[:, units:] = mm(held[...], up_w[...])
    if len(outs) == 1:
        outs[0][...] = sums[...].astype(jnp.bfloat16)
        return
    keep, away = outs[0], outs[1:]
    half, part = at // 2, away[0].shape[0]
    start = pl.multiple_of((1 - block[0]) * half, half)
    for index, out in enumerate(away):
        out[...] = sums[pl.ds(start + index * part, part), :].astype(jnp.bfloat16)
    keep[...] = sums[pl.ds(pl.multiple_of(block[0] * half, half), half), :]


def partial_units(split, block, pieces, gate_w, up_w):
    tokens = sum(piece.shape[0] for piece in pieces)
    features, units = gate_w.shape
    if split:
        out_shape = (
            jax.ShapeDtypeStruct((tokens // 2, 2 * units), jnp.float32),
            *[jax.ShapeDtypeStruct((tokens // 2 // split, 2 * units), jnp.bfloat16)] * split,
        )
    else:
        out_shape = (jax.ShapeDtypeStruct((tokens, 2 * units), jnp.bfloat16),)
    return pl.pallas_call(
        functools.partial(units_kernel, len(pieces)),
        out_shape=out_shape,
        in_specs=[SMEM] + [VMEM] * (len(pieces) + 2),
        out_specs=(VMEM,) * len(out_shape),
        scratch_shapes=[
            pltpu.VMEM((tokens, features), jnp.bfloat16),
            pltpu.VMEM((tokens, 2 * units), jnp.float32),
        ],
        compiler_params=pltpu.CompilerParams(vmem_limit_bytes=UNITS_VMEM),
        cost_estimate=pl.CostEstimate(
            flops=4 * tokens * features * units,
            bytes_accessed=2 * tokens * features + 4 * features * units,
            transcendentals=0,
        ),
        name="gate_up",
    )(block, *pieces, gate_w, up_w)


def hidden_kernel(n, *refs):
    sums, others, out = refs[:n], refs[n:-1], refs[-1]
    units = out.shape[1]
    both = jnp.concatenate([part[...].astype(jnp.float32) for part in sums], axis=0)
    if others:
        both = both + jnp.concatenate([part[...].astype(jnp.float32) for part in others], axis=0)
    gate, up = both[:, :units], both[:, units:]
    out[...] = (gate / (1.0 + jnp.exp(-gate)) * up).astype(jnp.bfloat16)


def hidden_units(sums, others=()):
    tokens, units = sum(part.shape[0] for part in sums), sums[0].shape[1] // 2
    return pl.pallas_call(
        functools.partial(hidden_kernel, len(sums)),
        out_shape=jax.ShapeDtypeStruct((tokens, units), jnp.bfloat16),
        in_specs=[VMEM] * (len(sums) + len(others)),
        out_specs=VMEM,
        compiler_params=pltpu.CompilerParams(vmem_limit_bytes=4 * MIB),
        name="hidden",
    )(*sums, *others)


def down_kernel(order, flip, n, chip_ref, core_ref, *refs):
    parts, source, middle, down_w = refs[:n], *refs[n : n + 3]
    keep, send, hidden = refs[n + 3], refs[n + 4], refs[-1]
    tokens = hidden.shape[0]
    rows = middle.shape[0]
    chip, core = chip_ref[0], core_ref[0]
    at = 0
    for part in parts:
        hidden[at : at + part.shape[0], :] = part[...]
        at += part.shape[0]
    wanted = []
    for side in (core, 1 - core):
        for dest in order:
            dest = dest ^ chip if flip else dest
            wanted.append(source[pl.ds(pl.multiple_of((2 * dest + side) * rows, rows), rows), :])
    wanted = jnp.concatenate(wanted, axis=0)
    slot, local = wanted[:, 0:1], wanted[:, 1:2]
    count = wanted.shape[0]
    pick = (lax.broadcasted_iota(jnp.int32, (count, tokens), 1) == slot).astype(jnp.bfloat16)
    moved = mm(pick, hidden[...]).astype(jnp.bfloat16)
    mine = lax.broadcasted_iota(jnp.int32, (count, rows), 1) == local
    mine = mine.astype(jnp.bfloat16)
    high = middle[...].astype(jnp.bfloat16)
    low = (middle[...] - high.astype(jnp.float32)).astype(jnp.bfloat16)
    term = mm(moved, down_w[...]) + (mm(mine, high) + mm(mine, low))
    keep[...] = term[: count // 2]
    send[...] = term[count // 2 :].astype(jnp.bfloat16)


def down(order, flip, chip, core, parts, source, middle, down_w):
    units, features = down_w.shape
    tokens, rows = source.shape[0], middle.shape[0]
    shape = (len(order) * rows, features)
    return pl.pallas_call(
        functools.partial(down_kernel, order, flip, len(parts)),
        out_shape=(
            jax.ShapeDtypeStruct(shape, jnp.float32),
            jax.ShapeDtypeStruct(shape, jnp.bfloat16),
        ),
        in_specs=[SMEM, SMEM] + [VMEM] * (len(parts) + 3),
        out_specs=(VMEM, VMEM),
        scratch_shapes=[pltpu.VMEM((tokens, units), jnp.bfloat16)],
        compiler_params=pltpu.CompilerParams(vmem_limit_bytes=DOWN_VMEM),
        name="down",
    )(chip, core, *parts, source, middle, down_w)


def pack_kernel(n, *refs):
    pieces, out = refs[:n], refs[-1]
    at = 0
    for piece in pieces:
        out[at : at + piece.shape[0], :] = piece[...]
        at += piece.shape[0]


def pack(pieces, after=()):
    rows = sum(piece.shape[0] for piece in pieces)
    return pl.pallas_call(
        functools.partial(pack_kernel, len(pieces)),
        out_shape=jax.ShapeDtypeStruct((rows, pieces[0].shape[1]), pieces[0].dtype),
        in_specs=[VMEM] * len(pieces) + [ANY] * len(after),
        out_specs=VMEM,
        compiler_params=pltpu.CompilerParams(vmem_limit_bytes=4 * MIB),
        name="pack",
    )(*pieces, *after)


def add_kernel(keep, other, *outs):
    at = 0
    for out in outs:
        to = at + out.shape[0]
        out[...] = (keep[at:to, :] + other[at:to, :].astype(jnp.float32)).astype(out.dtype)
        at = to


def add_parts(keep, other, kinds):
    rows, features = keep.shape
    return pl.pallas_call(
        add_kernel,
        out_shape=tuple(
            jax.ShapeDtypeStruct((rows // len(kinds), features), kind) for kind in kinds
        ),
        in_specs=[VMEM, VMEM],
        out_specs=(VMEM,) * len(kinds),
        compiler_params=pltpu.CompilerParams(vmem_limit_bytes=4 * MIB),
        name="add_parts",
    )(keep, other)


def finish_kernel(n, *refs):
    parts, gain, score, moved, stats = refs[:n], *refs[n:]
    total = functools.reduce(jnp.add, [part[...].astype(jnp.float32) for part in parts])
    moved[...] = total
    weighted = gain[...].astype(jnp.float32) * score[...].astype(jnp.float32)
    lane = lax.broadcasted_iota(jnp.int32, (total.shape[0], 128), 1)
    squares = jnp.sum(total * total, axis=1, keepdims=True)
    terms = jnp.sum(total * weighted, axis=1, keepdims=True)
    stats[...] = jnp.transpose(jnp.where(lane == 0, squares, terms))[:8]


def finish(parts, gain, score):
    rows, features = parts[0].shape
    return pl.pallas_call(
        functools.partial(finish_kernel, len(parts)),
        out_shape=(
            jax.ShapeDtypeStruct((rows, features), jnp.float32),
            jax.ShapeDtypeStruct((8, rows), jnp.float32),
        ),
        in_specs=[VMEM] * (len(parts) + 2),
        out_specs=(VMEM, VMEM),
        compiler_params=pltpu.CompilerParams(vmem_limit_bytes=4 * MIB),
        name="finish",
    )(*parts, gain, score)


def shards(
    n_chip,
    n_blk,
    resid,
    queries,
    new_kv,
    prefix_pool,
    page_table,
    prompt_len,
    tail_pool,
    tail_len,
    migration,
    out_w,
    mlp_gain,
    gate_w,
    up_w,
    down_w,
    final_gain,
    score_w,
):
    rows = resid.shape[0]
    features = gate_w.shape[0]
    chip = lax.axis_index("chip").astype(jnp.int32)
    core = lax.axis_index("core").astype(jnp.int32)
    block = lax.axis_index("blk").astype(jnp.int32)
    direct = n_chip == 8 and n_blk == 2

    def to_chip(value, index):
        return lax.ppermute(value, "chip", [(i, i ^ index) for i in range(n_chip)])

    def swap(value, axis):
        return lax.ppermute(value, axis, [(0, 1), (1, 0)])

    own, send = attention(
        queries, new_kv, prefix_pool, page_table, prompt_len, tail_pool, tail_len, out_w
    )
    if direct:
        own, other = own + resid.astype(jnp.float32), swap(send, "blk")
    else:
        own, other = resid.astype(jnp.float32), lax.psum(send, "blk")
    token = migration[:, None] * NEW + jnp.arange(NEW, dtype=jnp.int32)[None, :]
    token = token.reshape(-1, 1)
    came, inner = token // rows, token % rows
    far, far_core = (came // 2) ^ chip, (came % 2) ^ core
    if direct:
        held = far // 2 % 2
        one = (far_core ^ block) * 4 + held * 2
        two = 8 + (held ^ block) * 4 + far_core * 2
        slot = jnp.where(far % 2 == 0, one, two) + far // 4
    else:
        slot = far_core * n_chip + came // 2
    local = token - (chip * 2 + core) * rows
    source = jnp.concatenate([slot * rows + inner, local], axis=1)
    chip, core, block = (index.reshape(1) for index in (chip, core, block))
    gain_row, score_row = final_gain.reshape(1, -1), score_w.reshape(1, -1)

    normed, middle = normalize(
        block,
        own,
        other,
        mlp_gain,
        features,
        1 if direct else n_chip,
        (chip, core, source, gain_row, score_row),
    )
    if direct:
        piece = normed.reshape(rows, features)
        z2, z3, z1 = (to_chip(piece, index) for index in (4, 6, 2))
        here = [pack([piece, z2]), pack([z1, z3])]
        there = [to_chip(part, 1) for part in here]

        def summed(split, pieces):
            keep, *away = partial_units(split, block, pieces, gate_w, up_w)
            return keep, *[swap(part, "blk") for part in away]

        first = summed(2, here + [swap(part, "core") for part in here])
        near = pack(there, first[1:])
        second, third = summed(1, [near]), summed(1, [swap(near, "core")])
        hidden = hidden_units(first[:1], first[1:])
        parts = [hidden, swap(hidden, "blk")]
        hidden = hidden_units((second[0], third[0]), (second[1], third[1]))
        parts += [hidden, swap(hidden, "blk")]
    else:
        near = lax.all_to_all(normed, "chip", 0, 0).reshape(n_chip * rows, features)
        units = partial_units(0, block, [near, swap(near, "core")], gate_w, up_w)[0]
        parts = [hidden_units([lax.psum(units, "blk")])]
    if direct:
        near, wide = (
            down(order, True, chip, core, parts, source, middle, down_w)
            for order in ((0, 2, 1, 3), (6, 4, 7, 5))
        )
        kinds = (jnp.float32, jnp.bfloat16)
        near = add_parts(near[0], swap(near[1], "core"), kinds)
        wide = add_parts(wide[0], swap(wide[1], "core"), kinds)
        mine, to2 = add_parts(near[0], to_chip(near[1], 1), kinds)
        to6, to4 = add_parts(wide[0], to_chip(wide[1], 1), (jnp.bfloat16, jnp.bfloat16))
        sums = [mine, to_chip(to4, 4), to_chip(to6, 6), to_chip(to2, 2)]
    else:
        order = tuple(range(n_chip))
        keep, away = down(order, False, chip, core, parts, source, middle, down_w)
        total = (keep + swap(away, "core").astype(jnp.float32)).astype(jnp.bfloat16)
        total = lax.all_to_all(total.reshape(n_chip, rows, features), "chip", 0, 0)
        sums = [jnp.sum(total.astype(jnp.float32), axis=0)]
    moved, stats = finish(sums, gain_row, score_row)
    stats = stats + swap(stats, "blk") if direct else lax.psum(stats, "blk")
    score = stats[1] * lax.rsqrt(stats[0] / D + EPS)
    return (moved.astype(jnp.bfloat16), score)


def solution(mesh):
    n_chip, n_blk = mesh.shape["dp"] // 2, mesh.shape["blk"]
    split = Mesh(mesh.devices.reshape(n_chip, 2, n_blk), ("chip", "core", "blk"))
    dp = ("chip", "core")
    return jax.shard_map(
        functools.partial(shards, n_chip, n_blk),
        mesh=split,
        in_specs=(
            P(dp, None),
            P(dp, "blk", None),
            P(dp, None, "blk", None),
            P(dp, None, None, "blk", None),
            P(dp, None),
            P(dp),
            P(dp, None, None, "blk", None),
            P(dp, None),
            P(),
            P("blk", None),
            P(),
            P("blk", dp),
            P("blk", dp),
            P(dp, "blk"),
            P("blk"),
            P("blk"),
        ),
        out_specs=(P(dp, "blk"), P(dp)),
        check_vma=False,
    )
```

profile of v0, /device:TPU:0, one launch (start us, length us, event | category | flops | bytes accessed | tf_op | source)
XLA Modules:
  0.0 75.0 jit_solution(3872015854804645329)
XLA Ops:
  1.4 13.8 %attention.1 = (f32[32,2048]{1,0:T(8,128)}, bf16[32,2048]{1,0:T(8,128)(2,1)}) custom-call(s32[1,32]{1,0:T(1,128)} %table.1, s32[1]{0:T(128)S(6)} %copy.26.prompt_len, s32[1,16]{1,0:T(1,128)} %tail_len.1, bf16[256,128]{1,0:T(8,128)(2,1)} %bitcast.18, bf16[256,128]{1,0:T(8,128)(2,1)} %bitcast.19, bf16[32768,128]{1,0:T(8,128)(2,1)} %bitcast.16, ...), custom_call_target="tpu_custom_call" | custom-call | tf_op jit(solution)/shard_map/attention/pallas_call | solution.py:272
  15.1 3.0 %collective-permute-start = (bf16[32,2048]{1,0:T(8,128)(2,1)}, bf16[32,2048]{1,0:T(8,128)(2,1)S(1)}, u32[]{:S(2)}, u32[]{:S(2)}) collective-permute-start(bf16[32,2048]{1,0:T(8,128)(2,1)} %get-tuple-element.28), channel_id=1, source_target_pairs={{0,1},{1,0},{2,3},{3,2},{4,5},{5,4},{6,7},{7,6},{8,9},{9,8},{10,11... | collective-permute-start | bytes 393224 | tf_op jit(solution)/shard_map/ppermute | solution.py:568
  18.4 1.0 %convert_add_fusion.own = f32[32,2048]{1,0:T(8,128)S(1)} fusion(f32[32,2048]{1,0:T(8,128)} %get-tuple-element.27, bf16[32,2048]{1,0:T(8,128)(2,1)S(1)} %copy-done.3), kind=kLoop, calls=%fused_computation | loop fusion | flops 131072 | bytes 655360 | tf_op jit(solution)/shard_map/add | solution.py:574
  19.7 1.6 %collective-permute-done.other = bf16[32,2048]{1,0:T(8,128)(2,1)S(1)} collective-permute-done((bf16[32,2048]{1,0:T(8,128)(2,1)}, bf16[32,2048]{1,0:T(8,128)(2,1)S(1)}, u32[]{:S(2)}, u32[]{:S(2)}) %collective-permute-start) | collective-permute-done | bytes 131104 | tf_op jit(solution)/shard_map/ppermute | solution.py:568
  21.5 4.6 %collective-permute-start.3 = (bf16[32,1024]{1,0:T(8,128)(2,1)S(1)}, bf16[32,1024]{1,0:T(8,128)(2,1)S(1)}, u32[]{:S(2)}, u32[]{:S(2)}) collective-permute-start(bf16[32,1024]{1,0:T(8,128)(2,1)S(1)} %bitcast.12), channel_id=1, source_target_pairs={{0,24},{4,28},{8,16},{12,20},{16,8},{20,12},{24,0},{28,4},{1,25},{... | collective-permute-start | bytes 196616 | tf_op jit(solution)/shard_map/ppermute | solution.py:565
  26.1 3.7 %collective-permute-done.3.refs_1_ = bf16[32,1024]{1,0:T(8,128)(2,1)S(1)} collective-permute-done((bf16[32,1024]{1,0:T(8,128)(2,1)S(1)}, bf16[32,1024]{1,0:T(8,128)(2,1)S(1)}, u32[]{:S(2)}, u32[]{:S(2)}) %collective-permute-start.3) | collective-permute-done | bytes 65568 | tf_op jit(solution)/shard_map/ppermute | solution.py:565
  29.9 1.4 %collective-permute-done.1.refs_1_ = bf16[32,1024]{1,0:T(8,128)(2,1)S(1)} collective-permute-done((bf16[32,1024]{1,0:T(8,128)(2,1)S(1)}, bf16[32,1024]{1,0:T(8,128)(2,1)S(1)}, u32[]{:S(2)}, u32[]{:S(2)}) %collective-permute-start.1) | collective-permute-done | bytes 65568 | tf_op jit(solution)/shard_map/ppermute | solution.py:565
  31.4 1.5 %collective-permute-start.10 = (bf16[64,1024]{1,0:T(8,128)(2,1)S(1)}, bf16[64,1024]{1,0:T(8,128)(2,1)S(1)}, u32[]{:S(2)}, u32[]{:S(2)}) collective-permute-start(bf16[64,1024]{1,0:T(8,128)(2,1)S(1)} %pack.4.refs_1_), channel_id=1, source_target_pairs={{0,4},{4,0},{8,12},{12,8},{16,20},{20,16},{24,28},{28,24},{1,5},{5... | collective-permute-start | bytes 393224 | tf_op jit(solution)/shard_map/ppermute | solution.py:565
  33.5 0.7 gate_up.3
  34.3 1.6 %collective-permute-start.6 = (bf16[64,768]{1,0:T(8,128)(2,1)S(1)}, bf16[64,768]{1,0:T(8,128)(2,1)S(1)}, u32[]{:S(2)}, u32[]{:S(2)}) collective-permute-start(bf16[64,768]{1,0:T(8,128)(2,1)S(1)} %get-tuple-element.31), channel_id=1, source_target_pairs={{0,1},{1,0},{2,3},{3,2},{4,5},{5,4},{6,7},{7,6},{8,9},{9,8},{10,11... | collective-permute-start | bytes 294920 | tf_op jit(solution)/shard_map/ppermute | solution.py:568
  36.4 1.4 %collective-permute-done.10.refs_1_ = bf16[64,1024]{1,0:T(8,128)(2,1)S(1)} collective-permute-done((bf16[64,1024]{1,0:T(8,128)(2,1)S(1)}, bf16[64,1024]{1,0:T(8,128)(2,1)S(1)}, u32[]{:S(2)}, u32[]{:S(2)}) %collective-permute-start.10) | collective-permute-done | bytes 131104 | tf_op jit(solution)/shard_map/ppermute | solution.py:565
  37.8 2.4 %collective-permute-done.9.refs_0_ = bf16[64,1024]{1,0:T(8,128)(2,1)S(1)} collective-permute-done((bf16[64,1024]{1,0:T(8,128)(2,1)S(1)}, bf16[64,1024]{1,0:T(8,128)(2,1)S(1)}, u32[]{:S(2)}, u32[]{:S(2)}) %collective-permute-start.9) | collective-permute-done | bytes 131104 | tf_op jit(solution)/shard_map/ppermute | solution.py:565
  40.1 0.9 %collective-permute-done.7.refs_2_.refs_3_ = bf16[64,768]{1,0:T(8,128)(2,1)S(1)} collective-permute-done((bf16[64,768]{1,0:T(8,128)(2,1)S(1)}, bf16[64,768]{1,0:T(8,128)(2,1)S(1)}, u32[]{:S(2)}, u32[]{:S(2)}) %collective-permute-start.7) | collective-permute-done | bytes 98336 | tf_op jit(solution)/shard_map/ppermute | solution.py:568
  41.6 1.5 %collective-permute-start.12 = (bf16[64,768]{1,0:T(8,128)(2,1)S(1)}, bf16[64,768]{1,0:T(8,128)(2,1)S(1)}, u32[]{:S(2)}, u32[]{:S(2)}) collective-permute-start(bf16[64,768]{1,0:T(8,128)(2,1)S(1)} %get-tuple-element.35), channel_id=1, source_target_pairs={{0,1},{1,0},{2,3},{3,2},{4,5},{5,4},{6,7},{7,6},{8,9},{9,8},{10,11... | collective-permute-start | bytes 294920 | tf_op jit(solution)/shard_map/ppermute | solution.py:568
  43.6 1.1 %collective-permute-start.13 = (bf16[64,768]{1,0:T(8,128)(2,1)S(1)}, bf16[64,768]{1,0:T(8,128)(2,1)S(1)}, u32[]{:S(2)}, u32[]{:S(2)}) collective-permute-start(bf16[64,768]{1,0:T(8,128)(2,1)S(1)} %get-tuple-element.36), channel_id=1, source_target_pairs={{0,1},{1,0},{2,3},{3,2},{4,5},{5,4},{6,7},{7,6},{8,9},{9,8},{10,11... | collective-permute-start | bytes 294920 | tf_op jit(solution)/shard_map/ppermute | solution.py:568
  44.8 1.1 %collective-permute-start.8 = (bf16[128,384]{1,0:T(8,128)(2,1)S(1)}, bf16[128,384]{1,0:T(8,128)(2,1)S(1)}, u32[]{:S(2)}, u32[]{:S(2)}) collective-permute-start(bf16[128,384]{1,0:T(8,128)(2,1)S(1)} %hidden.2.refs_0_), channel_id=1, source_target_pairs={{0,1},{1,0},{2,3},{3,2},{4,5},{5,4},{6,7},{7,6},{8,9},{9,8},{10,11... | collective-permute-start | bytes 294920 | tf_op jit(solution)/shard_map/ppermute | solution.py:568
  45.9 1.4 %collective-permute-done.12.refs_2_ = bf16[64,768]{1,0:T(8,128)(2,1)S(1)} collective-permute-done((bf16[64,768]{1,0:T(8,128)(2,1)S(1)}, bf16[64,768]{1,0:T(8,128)(2,1)S(1)}, u32[]{:S(2)}, u32[]{:S(2)}) %collective-permute-start.12) | collective-permute-done | bytes 98336 | tf_op jit(solution)/shard_map/ppermute | solution.py:568
  47.3 2.1 %collective-permute-done.13.refs_3_ = bf16[64,768]{1,0:T(8,128)(2,1)S(1)} collective-permute-done((bf16[64,768]{1,0:T(8,128)(2,1)S(1)}, bf16[64,768]{1,0:T(8,128)(2,1)S(1)}, u32[]{:S(2)}, u32[]{:S(2)}) %collective-permute-start.13) | collective-permute-done | bytes 98336 | tf_op jit(solution)/shard_map/ppermute | solution.py:568
  49.5 1.6 %collective-permute-start.14 = (bf16[128,384]{1,0:T(8,128)(2,1)S(1)}, bf16[128,384]{1,0:T(8,128)(2,1)S(1)}, u32[]{:S(2)}, u32[]{:S(2)}) collective-permute-start(bf16[128,384]{1,0:T(8,128)(2,1)S(1)} %hidden.3.refs_2_), channel_id=1, source_target_pairs={{0,1},{1,0},{2,3},{3,2},{4,5},{5,4},{6,7},{7,6},{8,9},{9,8},{10,11... | collective-permute-start | bytes 294920 | tf_op jit(solution)/shard_map/ppermute | solution.py:568
  51.1 3.0 %collective-permute-done.14.refs_3_ = bf16[128,384]{1,0:T(8,128)(2,1)S(1)} collective-permute-done((bf16[128,384]{1,0:T(8,128)(2,1)S(1)}, bf16[128,384]{1,0:T(8,128)(2,1)S(1)}, u32[]{:S(2)}, u32[]{:S(2)}) %collective-permute-start.14) | collective-permute-done | bytes 98336 | tf_op jit(solution)/shard_map/ppermute | solution.py:568
  54.1 0.9 %down.3 = (f32[128,1024]{1,0:T(8,128)S(1)}, bf16[128,1024]{1,0:T(8,128)(2,1)S(1)}) custom-call(s32[1]{0:T(128)} %bitcast.refs_0_.chip_ref, s32[1]{0:T(128)} %bitcast.1.refs_1_.core_ref, bf16[128,384]{1,0:T(8,128)(2,1)S(1)} %hidden.2.refs_0_, bf16[128,384]{1,0:T(8,128)(2,1)S(1)} %collective-permute-done.8.refs_1_, bf16[128,384]{1,0:T(8,128)(2,1)S(1)} %hidden.3.refs_2_, ...), custom_call_target="tpu_custom_call" | custom-call | tf_op jit(solution)/shard_map/down/pallas_call | solution.py:455
  55.1 0.9 %down.2 = (f32[128,1024]{1,0:T(8,128)S(1)}, bf16[128,1024]{1,0:T(8,128)(2,1)S(1)}) custom-call(s32[1]{0:T(128)} %bitcast.refs_0_.chip_ref, s32[1]{0:T(128)} %bitcast.1.refs_1_.core_ref, bf16[128,384]{1,0:T(8,128)(2,1)S(1)} %hidden.2.refs_0_, bf16[128,384]{1,0:T(8,128)(2,1)S(1)} %collective-permute-done.8.refs_1_, bf16[128,384]{1,0:T(8,128)(2,1)S(1)} %hidden.3.refs_2_, ...), custom_call_target="tpu_custom_call" | custom-call | tf_op jit(solution)/shard_map/down/pallas_call | solution.py:455
  56.7 1.5 %collective-permute-start.18 = (bf16[64,1024]{1,0:T(8,128)(2,1)S(1)}, bf16[64,1024]{1,0:T(8,128)(2,1)S(1)}, u32[]{:S(2)}, u32[]{:S(2)}) collective-permute-start(bf16[64,1024]{1,0:T(8,128)(2,1)S(1)} %get-tuple-element.46), channel_id=1, source_target_pairs={{0,4},{4,0},{8,12},{12,8},{16,20},{20,16},{24,28},{28,24},{1,5},{5... | collective-permute-start | bytes 393224 | tf_op jit(solution)/shard_map/ppermute | solution.py:565
  58.3 1.1 %collective-permute-start.16 = (bf16[64,1024]{1,0:T(8,128)(2,1)S(1)}, bf16[64,1024]{1,0:T(8,128)(2,1)S(1)}, u32[]{:S(2)}, u32[]{:S(2)}) collective-permute-start(bf16[64,1024]{1,0:T(8,128)(2,1)S(1)} %get-tuple-element.41), channel_id=1, source_target_pairs={{0,4},{4,0},{8,12},{12,8},{16,20},{20,16},{24,28},{28,24},{1,5},{5... | collective-permute-start | bytes 393224 | tf_op jit(solution)/shard_map/ppermute | solution.py:565
  59.4 3.7 %collective-permute-done.18.other = bf16[64,1024]{1,0:T(8,128)(2,1)S(1)} collective-permute-done((bf16[64,1024]{1,0:T(8,128)(2,1)S(1)}, bf16[64,1024]{1,0:T(8,128)(2,1)S(1)}, u32[]{:S(2)}, u32[]{:S(2)}) %collective-permute-start.18) | collective-permute-done | bytes 131104 | tf_op jit(solution)/shard_map/ppermute | solution.py:565
  63.2 1.2 %collective-permute-start.19 = (bf16[32,1024]{1,0:T(8,128)(2,1)S(1)}, bf16[32,1024]{1,0:T(8,128)(2,1)S(1)}, u32[]{:S(2)}, u32[]{:S(2)}) collective-permute-start(bf16[32,1024]{1,0:T(8,128)(2,1)S(1)} %get-tuple-element.47), channel_id=1, source_target_pairs={{0,16},{4,20},{8,24},{12,28},{16,0},{20,4},{24,8},{28,12},{1,17},{... | collective-permute-start | bytes 196616 | tf_op jit(solution)/shard_map/ppermute | solution.py:565
  64.3 1.3 %collective-permute-start.20 = (bf16[32,1024]{1,0:T(8,128)(2,1)S(1)}, bf16[32,1024]{1,0:T(8,128)(2,1)S(1)}, u32[]{:S(2)}, u32[]{:S(2)}) collective-permute-start(bf16[32,1024]{1,0:T(8,128)(2,1)S(1)} %get-tuple-element.48), channel_id=1, source_target_pairs={{0,24},{4,28},{8,16},{12,20},{16,8},{20,12},{24,0},{28,4},{1,25},{... | collective-permute-start | bytes 196616 | tf_op jit(solution)/shard_map/ppermute | solution.py:565
  65.7 1.1 %collective-permute-start.21 = (bf16[32,1024]{1,0:T(8,128)(2,1)S(1)}, bf16[32,1024]{1,0:T(8,128)(2,1)S(1)}, u32[]{:S(2)}, u32[]{:S(2)}) collective-permute-start(bf16[32,1024]{1,0:T(8,128)(2,1)S(1)} %get-tuple-element.49), channel_id=1, source_target_pairs={{0,8},{4,12},{8,0},{12,4},{16,24},{20,28},{24,16},{28,20},{1,9},{5... | collective-permute-start | bytes 196616 | tf_op jit(solution)/shard_map/ppermute | solution.py:565
  66.8 2.4 %collective-permute-done.19.refs_1_ = bf16[32,1024]{1,0:T(8,128)(2,1)S(1)} collective-permute-done((bf16[32,1024]{1,0:T(8,128)(2,1)S(1)}, bf16[32,1024]{1,0:T(8,128)(2,1)S(1)}, u32[]{:S(2)}, u32[]{:S(2)}) %collective-permute-start.19) | collective-permute-done | bytes 65568 | tf_op jit(solution)/shard_map/ppermute | solution.py:565
  69.2 1.3 %collective-permute-done.20.refs_2_ = bf16[32,1024]{1,0:T(8,128)(2,1)S(1)} collective-permute-done((bf16[32,1024]{1,0:T(8,128)(2,1)S(1)}, bf16[32,1024]{1,0:T(8,128)(2,1)S(1)}, u32[]{:S(2)}, u32[]{:S(2)}) %collective-permute-start.20) | collective-permute-done | bytes 65568 | tf_op jit(solution)/shard_map/ppermute | solution.py:565
  70.9 1.6 %collective-permute-start.22 = (f32[8,32]{1,0:T(8,128)S(1)}, f32[8,32]{1,0:T(8,128)S(1)}, u32[]{:S(2)}, u32[]{:S(2)}) collective-permute-start(f32[8,32]{1,0:T(8,128)S(1)} %get-tuple-element.51), channel_id=1, source_target_pairs={{0,1},{1,0},{2,3},{3,2},{4,5},{5,4},{6,7},{7,6},{8,9},{9,8},{10,11... | collective-permute-start | bytes 3080 | tf_op jit(solution)/shard_map/ppermute | solution.py:568
  73.1 1.4 %collective-permute-done.22 = f32[8,32]{1,0:T(8,128)S(1)} collective-permute-done((f32[8,32]{1,0:T(8,128)S(1)}, f32[8,32]{1,0:T(8,128)S(1)}, u32[]{:S(2)}, u32[]{:S(2)}) %collective-permute-start.22) | collective-permute-done | bytes 1056 | tf_op jit(solution)/shard_map/ppermute | solution.py:568
  (60 shorter events, 5.6 us)
Async XLA Ops:
  1.3 16.8 %copy-start.7 = (s32[256]{0:T(256)S(1)}, s32[256]{0:T(256)}, u32[]{:S(2)}) copy-start(s32[256]{0:T(256)} %param.24) | copy-start | bytes 3076
  1.3 17.1 %copy-start.3 = (bf16[32,2048]{1,0:T(8,128)(2,1)S(1)}, bf16[32,2048]{1,0:T(8,128)(2,1)}, u32[]{:S(2)}) copy-start(bf16[32,2048]{1,0:T(8,128)(2,1)} %param.16) | copy-start | bytes 393220
  1.3 18.3 %copy-start.5 = (bf16[1024]{0:T(1024)(128)(2,1)S(1)}, bf16[1024]{0:T(1024)(128)(2,1)}, u32[]{:S(2)}) copy-start(bf16[1024]{0:T(1024)(128)(2,1)} %param.30) | copy-start | bytes 6148
  1.3 18.3 %copy-start.6 = (bf16[1024]{0:T(1024)(128)(2,1)S(1)}, bf16[1024]{0:T(1024)(128)(2,1)}, u32[]{:S(2)}) copy-start(bf16[1024]{0:T(1024)(128)(2,1)} %param.31) | copy-start | bytes 6148
  1.3 18.3 %copy-start.4 = (bf16[2048]{0:T(1024)(128)(2,1)S(1)}, bf16[2048]{0:T(1024)(128)(2,1)}, u32[]{:S(2)}) copy-start(bf16[2048]{0:T(1024)(128)(2,1)} %param.26) | copy-start | bytes 12292
  1.3 32.2 %copy-start = (bf16[1024,384]{1,0:T(8,128)(2,1)S(1)}, bf16[1024,384]{1,0:T(8,128)(2,1)}, u32[]{:S(2)}) copy-start(bf16[1024,384]{1,0:T(8,128)(2,1)} %refs_1_.3) | copy-start | bytes 2359300
  1.3 32.2 %copy-start.1 = (bf16[1024,384]{1,0:T(8,128)(2,1)S(1)}, bf16[1024,384]{1,0:T(8,128)(2,1)}, u32[]{:S(2)}) copy-start(bf16[1024,384]{1,0:T(8,128)(2,1)} %refs_2_.3) | copy-start | bytes 2359300
  15.1 6.2 %collective-permute-start = (bf16[32,2048]{1,0:T(8,128)(2,1)}, bf16[32,2048]{1,0:T(8,128)(2,1)S(1)}, u32[]{:S(2)}, u32[]{:S(2)}) collective-permute-start(bf16[32,2048]{1,0:T(8,128)(2,1)} %get-tuple-element.28), channel_id=1, source_target_pairs={{0,1},{1,0},{2,3},{3,2},{4,5},{5,4},{6,7},{7,6},{8,9},{9,8},{10,11... | collective-permute-start | bytes 393224 | tf_op jit(solution)/shard_map/ppermute | solution.py:568
  21.4 32.7 %copy-start.2 = (bf16[384,1024]{1,0:T(8,128)(2,1)S(1)}, bf16[384,1024]{1,0:T(8,128)(2,1)}, u32[]{:S(2)}) copy-start(bf16[384,1024]{1,0:T(8,128)(2,1)} %refs_6_.3) | copy-start | bytes 2359300
  21.4 4.7 %collective-permute-start.2 = (bf16[32,1024]{1,0:T(8,128)(2,1)S(1)}, bf16[32,1024]{1,0:T(8,128)(2,1)S(1)}, u32[]{:S(2)}, u32[]{:S(2)}) collective-permute-start(bf16[32,1024]{1,0:T(8,128)(2,1)S(1)} %bitcast.11), channel_id=1, source_target_pairs={{0,8},{4,12},{8,0},{12,4},{16,24},{20,28},{24,16},{28,20},{1,9},{5... | collective-permute-start | bytes 196616 | tf_op jit(solution)/shard_map/ppermute | solution.py:565
  21.5 8.3 %collective-permute-start.3 = (bf16[32,1024]{1,0:T(8,128)(2,1)S(1)}, bf16[32,1024]{1,0:T(8,128)(2,1)S(1)}, u32[]{:S(2)}, u32[]{:S(2)}) collective-permute-start(bf16[32,1024]{1,0:T(8,128)(2,1)S(1)} %bitcast.12), channel_id=1, source_target_pairs={{0,24},{4,28},{8,16},{12,20},{16,8},{20,12},{24,0},{28,4},{1,25},{... | collective-permute-start | bytes 196616 | tf_op jit(solution)/shard_map/ppermute | solution.py:565
  26.1 5.2 %collective-permute-start.1 = (bf16[32,1024]{1,0:T(8,128)(2,1)S(1)}, bf16[32,1024]{1,0:T(8,128)(2,1)S(1)}, u32[]{:S(2)}, u32[]{:S(2)}) collective-permute-start(bf16[32,1024]{1,0:T(8,128)(2,1)S(1)} %bitcast.13), channel_id=1, source_target_pairs={{0,16},{4,20},{8,24},{12,28},{16,0},{20,4},{24,8},{28,12},{1,17},{... | collective-permute-start | bytes 196616 | tf_op jit(solution)/shard_map/ppermute | solution.py:565
  29.8 3.7 %collective-permute-start.5 = (bf16[64,1024]{1,0:T(8,128)(2,1)S(1)}, bf16[64,1024]{1,0:T(8,128)(2,1)S(1)}, u32[]{:S(2)}, u32[]{:S(2)}) collective-permute-start(bf16[64,1024]{1,0:T(8,128)(2,1)S(1)} %pack.4.refs_1_), channel_id=1, source_target_pairs={{0,2},{2,0},{1,3},{3,1},{4,6},{6,4},{5,7},{7,5},{8,10},{10,8},{9,1... | collective-permute-start | bytes 393224 | tf_op jit(solution)/shard_map/ppermute | solution.py:568
  31.3 2.2 %collective-permute-start.4 = (bf16[64,1024]{1,0:T(8,128)(2,1)S(1)}, bf16[64,1024]{1,0:T(8,128)(2,1)S(1)}, u32[]{:S(2)}, u32[]{:S(2)}) collective-permute-start(bf16[64,1024]{1,0:T(8,128)(2,1)S(1)} %pack.3.refs_0_), channel_id=1, source_target_pairs={{0,2},{2,0},{1,3},{3,1},{4,6},{6,4},{5,7},{7,5},{8,10},{10,8},{9,1... | collective-permute-start | bytes 393224 | tf_op jit(solution)/shard_map/ppermute | solution.py:568
  31.4 6.4 %collective-permute-start.10 = (bf16[64,1024]{1,0:T(8,128)(2,1)S(1)}, bf16[64,1024]{1,0:T(8,128)(2,1)S(1)}, u32[]{:S(2)}, u32[]{:S(2)}) collective-permute-start(bf16[64,1024]{1,0:T(8,128)(2,1)S(1)} %pack.4.refs_1_), channel_id=1, source_target_pairs={{0,4},{4,0},{8,12},{12,8},{16,20},{20,16},{24,28},{28,24},{1,5},{5... | collective-permute-start | bytes 393224 | tf_op jit(solution)/shard_map/ppermute | solution.py:565
  32.9 7.2 %collective-permute-start.9 = (bf16[64,1024]{1,0:T(8,128)(2,1)S(1)}, bf16[64,1024]{1,0:T(8,128)(2,1)S(1)}, u32[]{:S(2)}, u32[]{:S(2)}) collective-permute-start(bf16[64,1024]{1,0:T(8,128)(2,1)S(1)} %pack.3.refs_0_), channel_id=1, source_target_pairs={{0,4},{4,0},{8,12},{12,8},{16,20},{20,16},{24,28},{28,24},{1,5},{5... | collective-permute-start | bytes 393224 | tf_op jit(solution)/shard_map/ppermute | solution.py:565
  34.3 5.9 %collective-permute-start.6 = (bf16[64,768]{1,0:T(8,128)(2,1)S(1)}, bf16[64,768]{1,0:T(8,128)(2,1)S(1)}, u32[]{:S(2)}, u32[]{:S(2)}) collective-permute-start(bf16[64,768]{1,0:T(8,128)(2,1)S(1)} %get-tuple-element.31), channel_id=1, source_target_pairs={{0,1},{1,0},{2,3},{3,2},{4,5},{5,4},{6,7},{7,6},{8,9},{9,8},{10,11... | collective-permute-start | bytes 294920 | tf_op jit(solution)/shard_map/ppermute | solution.py:568
  35.8 5.2 %collective-permute-start.7 = (bf16[64,768]{1,0:T(8,128)(2,1)S(1)}, bf16[64,768]{1,0:T(8,128)(2,1)S(1)}, u32[]{:S(2)}, u32[]{:S(2)}) collective-permute-start(bf16[64,768]{1,0:T(8,128)(2,1)S(1)} %get-tuple-element.32), channel_id=1, source_target_pairs={{0,1},{1,0},{2,3},{3,2},{4,5},{5,4},{6,7},{7,6},{8,9},{9,8},{10,11... | collective-permute-start | bytes 294920 | tf_op jit(solution)/shard_map/ppermute | solution.py:568
  41.1 2.1 %collective-permute-start.11 = (bf16[128,1024]{1,0:T(8,128)(2,1)S(1)}, bf16[128,1024]{1,0:T(8,128)(2,1)S(1)}, u32[]{:S(2)}, u32[]{:S(2)}) collective-permute-start(bf16[128,1024]{1,0:T(8,128)(2,1)S(1)} %pack.5.refs_0_), channel_id=1, source_target_pairs={{0,2},{2,0},{1,3},{3,1},{4,6},{6,4},{5,7},{7,5},{8,10},{10,8},{9,1... | collective-permute-start | bytes 786440 | tf_op jit(solution)/shard_map/ppermute | solution.py:568
  41.6 5.6 %collective-permute-start.12 = (bf16[64,768]{1,0:T(8,128)(2,1)S(1)}, bf16[64,768]{1,0:T(8,128)(2,1)S(1)}, u32[]{:S(2)}, u32[]{:S(2)}) collective-permute-start(bf16[64,768]{1,0:T(8,128)(2,1)S(1)} %get-tuple-element.35), channel_id=1, source_target_pairs={{0,1},{1,0},{2,3},{3,2},{4,5},{5,4},{6,7},{7,6},{8,9},{9,8},{10,11... | collective-permute-start | bytes 294920 | tf_op jit(solution)/shard_map/ppermute | solution.py:568
  43.6 5.7 %collective-permute-start.13 = (bf16[64,768]{1,0:T(8,128)(2,1)S(1)}, bf16[64,768]{1,0:T(8,128)(2,1)S(1)}, u32[]{:S(2)}, u32[]{:S(2)}) collective-permute-start(bf16[64,768]{1,0:T(8,128)(2,1)S(1)} %get-tuple-element.36), channel_id=1, source_target_pairs={{0,1},{1,0},{2,3},{3,2},{4,5},{5,4},{6,7},{7,6},{8,9},{9,8},{10,11... | collective-permute-start | bytes 294920 | tf_op jit(solution)/shard_map/ppermute | solution.py:568
  44.8 6.3 %collective-permute-start.8 = (bf16[128,384]{1,0:T(8,128)(2,1)S(1)}, bf16[128,384]{1,0:T(8,128)(2,1)S(1)}, u32[]{:S(2)}, u32[]{:S(2)}) collective-permute-start(bf16[128,384]{1,0:T(8,128)(2,1)S(1)} %hidden.2.refs_0_), channel_id=1, source_target_pairs={{0,1},{1,0},{2,3},{3,2},{4,5},{5,4},{6,7},{7,6},{8,9},{9,8},{10,11... | collective-permute-start | bytes 294920 | tf_op jit(solution)/shard_map/ppermute | solution.py:568
  49.5 4.7 %collective-permute-start.14 = (bf16[128,384]{1,0:T(8,128)(2,1)S(1)}, bf16[128,384]{1,0:T(8,128)(2,1)S(1)}, u32[]{:S(2)}, u32[]{:S(2)}) collective-permute-start(bf16[128,384]{1,0:T(8,128)(2,1)S(1)} %hidden.3.refs_2_), channel_id=1, source_target_pairs={{0,1},{1,0},{2,3},{3,2},{4,5},{5,4},{6,7},{7,6},{8,9},{9,8},{10,11... | collective-permute-start | bytes 294920 | tf_op jit(solution)/shard_map/ppermute | solution.py:568
  55.1 1.6 %collective-permute-start.17 = (bf16[128,1024]{1,0:T(8,128)(2,1)S(1)}, bf16[128,1024]{1,0:T(8,128)(2,1)S(1)}, u32[]{:S(2)}, u32[]{:S(2)}) collective-permute-start(bf16[128,1024]{1,0:T(8,128)(2,1)S(1)} %get-tuple-element.44), channel_id=1, source_target_pairs={{0,2},{2,0},{1,3},{3,1},{4,6},{6,4},{5,7},{7,5},{8,10},{10,8},{9,1... | collective-permute-start | bytes 786440 | tf_op jit(solution)/shard_map/ppermute | solution.py:568
  56.1 2.1 %collective-permute-start.15 = (bf16[128,1024]{1,0:T(8,128)(2,1)S(1)}, bf16[128,1024]{1,0:T(8,128)(2,1)S(1)}, u32[]{:S(2)}, u32[]{:S(2)}) collective-permute-start(bf16[128,1024]{1,0:T(8,128)(2,1)S(1)} %get-tuple-element.39), channel_id=1, source_target_pairs={{0,2},{2,0},{1,3},{3,1},{4,6},{6,4},{5,7},{7,5},{8,10},{10,8},{9,1... | collective-permute-start | bytes 786440 | tf_op jit(solution)/shard_map/ppermute | solution.py:568
  56.7 6.4 %collective-permute-start.18 = (bf16[64,1024]{1,0:T(8,128)(2,1)S(1)}, bf16[64,1024]{1,0:T(8,128)(2,1)S(1)}, u32[]{:S(2)}, u32[]{:S(2)}) collective-permute-start(bf16[64,1024]{1,0:T(8,128)(2,1)S(1)} %get-tuple-element.46), channel_id=1, source_target_pairs={{0,4},{4,0},{8,12},{12,8},{16,20},{20,16},{24,28},{28,24},{1,5},{5... | collective-permute-start | bytes 393224 | tf_op jit(solution)/shard_map/ppermute | solution.py:565
  58.3 7.4 %collective-permute-start.16 = (bf16[64,1024]{1,0:T(8,128)(2,1)S(1)}, bf16[64,1024]{1,0:T(8,128)(2,1)S(1)}, u32[]{:S(2)}, u32[]{:S(2)}) collective-permute-start(bf16[64,1024]{1,0:T(8,128)(2,1)S(1)} %get-tuple-element.41), channel_id=1, source_target_pairs={{0,4},{4,0},{8,12},{12,8},{16,20},{20,16},{24,28},{28,24},{1,5},{5... | collective-permute-start | bytes 393224 | tf_op jit(solution)/shard_map/ppermute | solution.py:565
  63.2 6.0 %collective-permute-start.19 = (bf16[32,1024]{1,0:T(8,128)(2,1)S(1)}, bf16[32,1024]{1,0:T(8,128)(2,1)S(1)}, u32[]{:S(2)}, u32[]{:S(2)}) collective-permute-start(bf16[32,1024]{1,0:T(8,128)(2,1)S(1)} %get-tuple-element.47), channel_id=1, source_target_pairs={{0,16},{4,20},{8,24},{12,28},{16,0},{20,4},{24,8},{28,12},{1,17},{... | collective-permute-start | bytes 196616 | tf_op jit(solution)/shard_map/ppermute | solution.py:565
  64.3 6.2 %collective-permute-start.20 = (bf16[32,1024]{1,0:T(8,128)(2,1)S(1)}, bf16[32,1024]{1,0:T(8,128)(2,1)S(1)}, u32[]{:S(2)}, u32[]{:S(2)}) collective-permute-start(bf16[32,1024]{1,0:T(8,128)(2,1)S(1)} %get-tuple-element.48), channel_id=1, source_target_pairs={{0,24},{4,28},{8,16},{12,20},{16,8},{20,12},{24,0},{28,4},{1,25},{... | collective-permute-start | bytes 196616 | tf_op jit(solution)/shard_map/ppermute | solution.py:565
  65.7 5.0 %collective-permute-start.21 = (bf16[32,1024]{1,0:T(8,128)(2,1)S(1)}, bf16[32,1024]{1,0:T(8,128)(2,1)S(1)}, u32[]{:S(2)}, u32[]{:S(2)}) collective-permute-start(bf16[32,1024]{1,0:T(8,128)(2,1)S(1)} %get-tuple-element.49), channel_id=1, source_target_pairs={{0,8},{4,12},{8,0},{12,4},{16,24},{20,28},{24,16},{28,20},{1,9},{5... | collective-permute-start | bytes 196616 | tf_op jit(solution)/shard_map/ppermute | solution.py:565
  70.9 3.6 %collective-permute-start.22 = (f32[8,32]{1,0:T(8,128)S(1)}, f32[8,32]{1,0:T(8,128)S(1)}, u32[]{:S(2)}, u32[]{:S(2)}) collective-permute-start(f32[8,32]{1,0:T(8,128)S(1)} %get-tuple-element.51), channel_id=1, source_target_pairs={{0,1},{1,0},{2,3},{3,2},{4,5},{5,4},{6,7},{7,6},{8,9},{9,8},{10,11... | collective-permute-start | bytes 3080 | tf_op jit(solution)/shard_map/ppermute | solution.py:568
where the time goes:
time: 75.5 us; the launch traced here: 75 us
  waiting for transfers between devices  27.2 us (36%)
  starting transfers between devices  25.7 us (34%)
  Pallas kernels  18 us (24%)
  other arithmetic  2.33 us (3%)
  between operations  1.59 us (2%)
    ppermute x10, waiting for transfers between devices, to_chip(): return lax.ppermute(value, 'chip', [(i, i ^ index) for i in range(n_chip)])  16.5 us
    pallas_call x1, Pallas kernels, attention(): pl.pallas_call(functools.partial(attention_kernel, (rows, heads, groups,...  13.8 us
    ppermute x10, starting transfers between devices, to_chip(): return lax.ppermute(value, 'chip', [(i, i ^ index) for i in range(n_chip)])  13 us
    ppermute x13, starting transfers between devices, swap(): return lax.ppermute(value, axis, [(0, 1), (1, 0)])  12.7 us
    ppermute x13, waiting for transfers between devices, swap(): return lax.ppermute(value, axis, [(0, 1), (1, 0)])  10.6 us
    pallas_call x2, Pallas kernels, down(): pl.pallas_call(functools.partial(down_kernel, order, flip, len(parts)), o...  1.86 us
    pallas_call x3, Pallas kernels, partial_units(): pl.pallas_call(functools.partial(units_kernel, len(pieces)), out_shape=ou...  1.67 us
  transfers between devices with their start and end apart: 23, of which 15 were waited for; matrix products, arithmetic and copies ran while one was open for 3% of the time, Pallas kernels for 4%

commit v1 on v0

--- a/solution.py
+++ b/solution.py
@@ -120,7 +120,7 @@
     sort = (came == (to % tokens) * step + to // tokens).astype(jnp.bfloat16)
 
     def take_apart(buf, start, count, outs, places):
-        for two in range(count // (2 * block)):
+        def one(two):
             x0 = buf[pl.ds(start + two * 2 * block, block), :]
             x1 = buf[pl.ds(start + (two * 2 + 1) * block, block), :]
             y = mm(sort, jnp.concatenate([x0, x1], axis=1)).astype(jnp.bfloat16)
@@ -132,6 +132,16 @@
                     outs[kind][g // pair, t, lane : lane + width] = y[
                         j * tokens : (j + 1) * tokens, side * width : (side + 1) * width
                     ]
+
+        return [functools.partial(one, two) for two in range(count // (2 * block))]
+
+    def alternate(works, others):
+        shares = len(others) or 1
+        for index in range(shares):
+            for work in works[index * len(works) // shares : (index + 1) * len(works) // shares]:
+                work()
+            if others:
+                others[index]()
 
     def blocks(x):
         return [x[:, i * 128 : (i + 1) * 128] for i in range(x.shape[1] // 128)]
@@ -175,9 +185,7 @@
     quad_key = lax.broadcasted_iota(jnp.int32, (8, quad_keys), 1)
     for index in range(quads):
         tail_copy(index).wait()
-    for index in range(quads):
-        outs, at = (tail_keys, tail_apart), index * quad_keys
-        take_apart(tail_buf, index * quad_rows, quad_rows, outs, (at, at))
+    def score_tails(index, n):
         reach = jnp.zeros((8, quad_keys), jnp.int32)
         for c in range(quad):
             reach = jnp.where(
@@ -186,14 +194,20 @@
         ok = (quad_row // NEW == quad_key // tail) & (quad_key < reach)
         ok = jnp.concatenate([ok] * (pair * repeat), axis=0)
         keys = slice(index * quad_keys, (index + 1) * quad_keys)
-        for n in range(pairs):
-            q = jnp.concatenate([q_rows[n, a, :] for a in quad_places(index)], axis=0)
-            s = mm_t(q.astype(jnp.bfloat16), tail_keys[n, keys, :]) * factor
-            s = jnp.where(ok, s, NEG)
-            tail_scores[n, index] = s
-            high = functools.reduce(jnp.maximum, blocks(s))
-            for i, a in enumerate(quad_places(index)):
-                top[n, a, :] = jnp.maximum(top[n, a, :], high[i * 8 : (i + 1) * 8])
+        q = jnp.concatenate([q_rows[n, a, :] for a in quad_places(index)], axis=0)
+        s = mm_t(q.astype(jnp.bfloat16), tail_keys[n, keys, :]) * factor
+        s = jnp.where(ok, s, NEG)
+        tail_scores[n, index] = s
+        high = functools.reduce(jnp.maximum, blocks(s))
+        for i, a in enumerate(quad_places(index)):
+            top[n, a, :] = jnp.maximum(top[n, a, :], high[i * 8 : (i + 1) * 8])
+
+    others = []
+    for index in range(quads):
+        outs, at = (tail_keys, tail_apart), index * quad_keys
+        alternate(take_apart(tail_buf, index * quad_rows, quad_rows, outs, (at, at)), others)
+        others = [functools.partial(score_tails, index, n) for n in range(pairs)]
+    alternate([], others)
 
     part = min(256, chunk)
     place = lax.broadcasted_iota(jnp.int32, (8, part), 1)
@@ -204,15 +218,20 @@
             page_copy(index * chunk_pages + i).wait()
         first = pl.multiple_of(index * chunk, chunk)
         row = pl.multiple_of(index * chunk_rows, chunk_rows)
+
+        def score(at, n):
+            ok = place[0:1] < length - (index * chunk + at)
+            s = mm_t(q_pairs[n], keys_apart[n, at : at + part, :]) * factor
+            s = jnp.where(ok, s, NEG)
+            scores[n, :, pl.ds(first + at, part)] = s
+            top[n] = functools.reduce(jnp.maximum, blocks(s), top[n])
+
+        others = []
         for at in range(0, chunk, part):
             outs, places = (keys_apart, apart), (at, first + at)
-            take_apart(pages, row + at * step, part * step, outs, places)
-            ok = place[0:1] < length - (index * chunk + at)
-            for n in range(pairs):
-                s = mm_t(q_pairs[n], keys_apart[n, at : at + part, :]) * factor
-                s = jnp.where(ok, s, NEG)
-                scores[n, :, pl.ds(first + at, part)] = s
-                top[n] = functools.reduce(jnp.maximum, blocks(s), top[n])
+            alternate(take_apart(pages, row + at * step, part * step, outs, places), others)
+            others = [functools.partial(score, at, n) for n in range(pairs)]
+        alternate([], others)
 
     for n in range(pairs):
         high = jnp.broadcast_to(jnp.max(top[n], axis=1, keepdims=True), top.shape[1:])

time: 75.5 us -> 74 us (0.980)
  Pallas kernels: 18 us -> 13.9 us
  waiting for transfers between devices: 27.2 us -> 28.6 us
  starting transfers between devices: 25.7 us -> 26.8 us
    pallas_call x1, Pallas kernels: 13.8 us -> 9.67 us  [attention(): pl.pallas_call(functools.partial(attention_kernel, (rows, heads, groups,...]
    ppermute x10, waiting for transfers between devices: 16.5 us -> 17.9 us  [to_chip(): return lax.ppermute(value, 'chip', [(i, i ^ index) for i in range(n_chip)])]
    ppermute x10, starting transfers between devices: 13 us -> 14.1 us  [to_chip(): return lax.ppermute(value, 'chip', [(i, i ^ index) for i in range(n_chip)])]
  transfers between devices with their start and end apart: 23 -> 23, of which waited for: 15 -> 17; matrix products, arithmetic and copies ran while one was open for 3% -> 3% of each run, Pallas kernels for 4% -> 4%
where the time goes in v1:
time: 74 us; the launch traced here: 73.5 us
  waiting for transfers between devices  28.6 us (39%)
  starting transfers between devices  26.8 us (36%)
  Pallas kernels  13.9 us (19%)
  other arithmetic  2.33 us (3%)
  between operations  1.58 us (2%)
    ppermute x10, waiting for transfers between devices, to_chip(): return lax.ppermute(value, 'chip', [(i, i ^ index) for i in range(n_chip)])  17.9 us
    ppermute x10, starting transfers between devices, to_chip(): return lax.ppermute(value, 'chip', [(i, i ^ index) for i in range(n_chip)])  14.1 us
    ppermute x13, starting transfers between devices, swap(): return lax.ppermute(value, axis, [(0, 1), (1, 0)])  12.7 us
    ppermute x13, waiting for transfers between devices, swap(): return lax.ppermute(value, axis, [(0, 1), (1, 0)])  10.7 us
    pallas_call x1, Pallas kernels, attention(): pl.pallas_call(functools.partial(attention_kernel, (rows, heads, groups,...  9.67 us
    pallas_call x2, Pallas kernels, down(): pl.pallas_call(functools.partial(down_kernel, order, flip, len(parts)), o...  1.85 us
    pallas_call x3, Pallas kernels, partial_units(): pl.pallas_call(functools.partial(units_kernel, len(pieces)), out_shape=ou...  1.67 us
  transfers between devices with their start and end apart: 23, of which 17 were waited for; matrix products, arithmetic and copies ran while one was open for 3% of the time, Pallas kernels for 4%

profile of v1, /device:TPU:0, one launch (start us, length us, event | category | flops | bytes accessed | tf_op | source)
XLA Modules:
  0.0 73.5 jit_solution(10220098019891583560)
XLA Ops:
  1.4 9.7 %attention.1 = (f32[32,2048]{1,0:T(8,128)}, bf16[32,2048]{1,0:T(8,128)(2,1)}) custom-call(s32[1,32]{1,0:T(1,128)} %table.1, s32[1]{0:T(128)S(6)} %copy.26.prompt_len, s32[1,16]{1,0:T(1,128)} %tail_len.1, bf16[256,128]{1,0:T(8,128)(2,1)} %bitcast.18, bf16[256,128]{1,0:T(8,128)(2,1)} %bitcast.19, bf16[32768,128]{1,0:T(8,128)(2,1)} %bitcast.16, ...), custom_call_target="tpu_custom_call" | custom-call | tf_op jit(solution)/shard_map/attention/pallas_call | solution.py:291
  11.0 3.0 %collective-permute-start = (bf16[32,2048]{1,0:T(8,128)(2,1)}, bf16[32,2048]{1,0:T(8,128)(2,1)S(1)}, u32[]{:S(2)}, u32[]{:S(2)}) collective-permute-start(bf16[32,2048]{1,0:T(8,128)(2,1)} %get-tuple-element.28), channel_id=1, source_target_pairs={{0,1},{1,0},{2,3},{3,2},{4,5},{5,4},{6,7},{7,6},{8,9},{9,8},{10,11... | collective-permute-start | bytes 393224 | tf_op jit(solution)/shard_map/ppermute | solution.py:587
  14.3 1.0 %convert_add_fusion.own = f32[32,2048]{1,0:T(8,128)S(1)} fusion(f32[32,2048]{1,0:T(8,128)} %get-tuple-element.27, bf16[32,2048]{1,0:T(8,128)(2,1)S(1)} %copy-done.3), kind=kLoop, calls=%fused_computation | loop fusion | flops 131072 | bytes 655360 | tf_op jit(solution)/shard_map/add | solution.py:593
  15.6 1.6 %collective-permute-done.other = bf16[32,2048]{1,0:T(8,128)(2,1)S(1)} collective-permute-done((bf16[32,2048]{1,0:T(8,128)(2,1)}, bf16[32,2048]{1,0:T(8,128)(2,1)S(1)}, u32[]{:S(2)}, u32[]{:S(2)}) %collective-permute-start) | collective-permute-done | bytes 131104 | tf_op jit(solution)/shard_map/ppermute | solution.py:587
  17.4 4.8 %collective-permute-start.2 = (bf16[32,1024]{1,0:T(8,128)(2,1)S(1)}, bf16[32,1024]{1,0:T(8,128)(2,1)S(1)}, u32[]{:S(2)}, u32[]{:S(2)}) collective-permute-start(bf16[32,1024]{1,0:T(8,128)(2,1)S(1)} %bitcast.11), channel_id=1, source_target_pairs={{0,8},{4,12},{8,0},{12,4},{16,24},{20,28},{24,16},{28,20},{1,9},{5... | collective-permute-start | bytes 196616 | tf_op jit(solution)/shard_map/ppermute | solution.py:584
  22.3 1.4 %collective-permute-start.1 = (bf16[32,1024]{1,0:T(8,128)(2,1)S(1)}, bf16[32,1024]{1,0:T(8,128)(2,1)S(1)}, u32[]{:S(2)}, u32[]{:S(2)}) collective-permute-start(bf16[32,1024]{1,0:T(8,128)(2,1)S(1)} %bitcast.13), channel_id=1, source_target_pairs={{0,16},{4,20},{8,24},{12,28},{16,0},{20,4},{24,8},{28,12},{1,17},{... | collective-permute-start | bytes 196616 | tf_op jit(solution)/shard_map/ppermute | solution.py:584
  23.7 0.9 %collective-permute-done.2.refs_0_ = bf16[32,1024]{1,0:T(8,128)(2,1)S(1)} collective-permute-done((bf16[32,1024]{1,0:T(8,128)(2,1)S(1)}, bf16[32,1024]{1,0:T(8,128)(2,1)S(1)}, u32[]{:S(2)}, u32[]{:S(2)}) %collective-permute-start.2) | collective-permute-done | bytes 65568 | tf_op jit(solution)/shard_map/ppermute | solution.py:584
  24.6 3.7 %collective-permute-done.3.refs_1_ = bf16[32,1024]{1,0:T(8,128)(2,1)S(1)} collective-permute-done((bf16[32,1024]{1,0:T(8,128)(2,1)S(1)}, bf16[32,1024]{1,0:T(8,128)(2,1)S(1)}, u32[]{:S(2)}, u32[]{:S(2)}) %collective-permute-start.3) | collective-permute-done | bytes 65568 | tf_op jit(solution)/shard_map/ppermute | solution.py:584
  28.4 1.7 %collective-permute-done.1.refs_1_ = bf16[32,1024]{1,0:T(8,128)(2,1)S(1)} collective-permute-done((bf16[32,1024]{1,0:T(8,128)(2,1)S(1)}, bf16[32,1024]{1,0:T(8,128)(2,1)S(1)}, u32[]{:S(2)}, u32[]{:S(2)}) %collective-permute-start.1) | collective-permute-done | bytes 65568 | tf_op jit(solution)/shard_map/ppermute | solution.py:584
  30.2 1.0 %collective-permute-start.10 = (bf16[64,1024]{1,0:T(8,128)(2,1)S(1)}, bf16[64,1024]{1,0:T(8,128)(2,1)S(1)}, u32[]{:S(2)}, u32[]{:S(2)}) collective-permute-start(bf16[64,1024]{1,0:T(8,128)(2,1)S(1)} %pack.4.refs_1_), channel_id=1, source_target_pairs={{0,4},{4,0},{8,12},{12,8},{16,20},{20,16},{24,28},{28,24},{1,5},{5... | collective-permute-start | bytes 393224 | tf_op jit(solution)/shard_map/ppermute | solution.py:584
  31.2 1.1 %collective-permute-start.9 = (bf16[64,1024]{1,0:T(8,128)(2,1)S(1)}, bf16[64,1024]{1,0:T(8,128)(2,1)S(1)}, u32[]{:S(2)}, u32[]{:S(2)}) collective-permute-start(bf16[64,1024]{1,0:T(8,128)(2,1)S(1)} %pack.3.refs_0_), channel_id=1, source_target_pairs={{0,4},{4,0},{8,12},{12,8},{16,20},{20,16},{24,28},{28,24},{1,5},{5... | collective-permute-start | bytes 393224 | tf_op jit(solution)/shard_map/ppermute | solution.py:584
  33.1 1.6 %collective-permute-start.6 = (bf16[64,768]{1,0:T(8,128)(2,1)S(1)}, bf16[64,768]{1,0:T(8,128)(2,1)S(1)}, u32[]{:S(2)}, u32[]{:S(2)}) collective-permute-start(bf16[64,768]{1,0:T(8,128)(2,1)S(1)} %get-tuple-element.31), channel_id=1, source_target_pairs={{0,1},{1,0},{2,3},{3,2},{4,5},{5,4},{6,7},{7,6},{8,9},{9,8},{10,11... | collective-permute-start | bytes 294920 | tf_op jit(solution)/shard_map/ppermute | solution.py:587
  35.2 1.4 %collective-permute-done.10.refs_1_ = bf16[64,1024]{1,0:T(8,128)(2,1)S(1)} collective-permute-done((bf16[64,1024]{1,0:T(8,128)(2,1)S(1)}, bf16[64,1024]{1,0:T(8,128)(2,1)S(1)}, u32[]{:S(2)}, u32[]{:S(2)}) %collective-permute-start.10) | collective-permute-done | bytes 131104 | tf_op jit(solution)/shard_map/ppermute | solution.py:584
  36.6 2.4 %collective-permute-done.9.refs_0_ = bf16[64,1024]{1,0:T(8,128)(2,1)S(1)} collective-permute-done((bf16[64,1024]{1,0:T(8,128)(2,1)S(1)}, bf16[64,1024]{1,0:T(8,128)(2,1)S(1)}, u32[]{:S(2)}, u32[]{:S(2)}) %collective-permute-start.9) | collective-permute-done | bytes 131104 | tf_op jit(solution)/shard_map/ppermute | solution.py:584
  38.9 0.9 %collective-permute-done.7.refs_2_.refs_3_ = bf16[64,768]{1,0:T(8,128)(2,1)S(1)} collective-permute-done((bf16[64,768]{1,0:T(8,128)(2,1)S(1)}, bf16[64,768]{1,0:T(8,128)(2,1)S(1)}, u32[]{:S(2)}, u32[]{:S(2)}) %collective-permute-start.7) | collective-permute-done | bytes 98336 | tf_op jit(solution)/shard_map/ppermute | solution.py:587
  40.4 1.5 %collective-permute-start.12 = (bf16[64,768]{1,0:T(8,128)(2,1)S(1)}, bf16[64,768]{1,0:T(8,128)(2,1)S(1)}, u32[]{:S(2)}, u32[]{:S(2)}) collective-permute-start(bf16[64,768]{1,0:T(8,128)(2,1)S(1)} %get-tuple-element.35), channel_id=1, source_target_pairs={{0,1},{1,0},{2,3},{3,2},{4,5},{5,4},{6,7},{7,6},{8,9},{9,8},{10,11... | collective-permute-start | bytes 294920 | tf_op jit(solution)/shard_map/ppermute | solution.py:587
  42.4 1.0 %collective-permute-start.13 = (bf16[64,768]{1,0:T(8,128)(2,1)S(1)}, bf16[64,768]{1,0:T(8,128)(2,1)S(1)}, u32[]{:S(2)}, u32[]{:S(2)}) collective-permute-start(bf16[64,768]{1,0:T(8,128)(2,1)S(1)} %get-tuple-element.36), channel_id=1, source_target_pairs={{0,1},{1,0},{2,3},{3,2},{4,5},{5,4},{6,7},{7,6},{8,9},{9,8},{10,11... | collective-permute-start | bytes 294920 | tf_op jit(solution)/shard_map/ppermute | solution.py:587
  43.6 1.1 %collective-permute-start.8 = (bf16[128,384]{1,0:T(8,128)(2,1)S(1)}, bf16[128,384]{1,0:T(8,128)(2,1)S(1)}, u32[]{:S(2)}, u32[]{:S(2)}) collective-permute-start(bf16[128,384]{1,0:T(8,128)(2,1)S(1)} %hidden.2.refs_0_), channel_id=1, source_target_pairs={{0,1},{1,0},{2,3},{3,2},{4,5},{5,4},{6,7},{7,6},{8,9},{9,8},{10,11... | collective-permute-start | bytes 294920 | tf_op jit(solution)/shard_map/ppermute | solution.py:587
  44.7 1.3 %collective-permute-done.12.refs_2_ = bf16[64,768]{1,0:T(8,128)(2,1)S(1)} collective-permute-done((bf16[64,768]{1,0:T(8,128)(2,1)S(1)}, bf16[64,768]{1,0:T(8,128)(2,1)S(1)}, u32[]{:S(2)}, u32[]{:S(2)}) %collective-permute-start.12) | collective-permute-done | bytes 98336 | tf_op jit(solution)/shard_map/ppermute | solution.py:587
  46.0 2.1 %collective-permute-done.13.refs_3_ = bf16[64,768]{1,0:T(8,128)(2,1)S(1)} collective-permute-done((bf16[64,768]{1,0:T(8,128)(2,1)S(1)}, bf16[64,768]{1,0:T(8,128)(2,1)S(1)}, u32[]{:S(2)}, u32[]{:S(2)}) %collective-permute-start.13) | collective-permute-done | bytes 98336 | tf_op jit(solution)/shard_map/ppermute | solution.py:587
  48.2 1.6 %collective-permute-start.14 = (bf16[128,384]{1,0:T(8,128)(2,1)S(1)}, bf16[128,384]{1,0:T(8,128)(2,1)S(1)}, u32[]{:S(2)}, u32[]{:S(2)}) collective-permute-start(bf16[128,384]{1,0:T(8,128)(2,1)S(1)} %hidden.3.refs_2_), channel_id=1, source_target_pairs={{0,1},{1,0},{2,3},{3,2},{4,5},{5,4},{6,7},{7,6},{8,9},{9,8},{10,11... | collective-permute-start | bytes 294920 | tf_op jit(solution)/shard_map/ppermute | solution.py:587
  49.9 3.0 %collective-permute-done.14.refs_3_ = bf16[128,384]{1,0:T(8,128)(2,1)S(1)} collective-permute-done((bf16[128,384]{1,0:T(8,128)(2,1)S(1)}, bf16[128,384]{1,0:T(8,128)(2,1)S(1)}, u32[]{:S(2)}, u32[]{:S(2)}) %collective-permute-start.14) | collective-permute-done | bytes 98336 | tf_op jit(solution)/shard_map/ppermute | solution.py:587
  52.9 0.9 %down.3 = (f32[128,1024]{1,0:T(8,128)S(1)}, bf16[128,1024]{1,0:T(8,128)(2,1)S(1)}) custom-call(s32[1]{0:T(128)} %bitcast.refs_0_.chip_ref, s32[1]{0:T(128)} %bitcast.1.refs_1_.core_ref, bf16[128,384]{1,0:T(8,128)(2,1)S(1)} %hidden.2.refs_0_, bf16[128,384]{1,0:T(8,128)(2,1)S(1)} %collective-permute-done.8.refs_1_, bf16[128,384]{1,0:T(8,128)(2,1)S(1)} %hidden.3.refs_2_, ...), custom_call_target="tpu_custom_call" | custom-call | tf_op jit(solution)/shard_map/down/pallas_call | solution.py:474
  53.9 0.9 %down.2 = (f32[128,1024]{1,0:T(8,128)S(1)}, bf16[128,1024]{1,0:T(8,128)(2,1)S(1)}) custom-call(s32[1]{0:T(128)} %bitcast.refs_0_.chip_ref, s32[1]{0:T(128)} %bitcast.1.refs_1_.core_ref, bf16[128,384]{1,0:T(8,128)(2,1)S(1)} %hidden.2.refs_0_, bf16[128,384]{1,0:T(8,128)(2,1)S(1)} %collective-permute-done.8.refs_1_, bf16[128,384]{1,0:T(8,128)(2,1)S(1)} %hidden.3.refs_2_, ...), custom_call_target="tpu_custom_call" | custom-call | tf_op jit(solution)/shard_map/down/pallas_call | solution.py:474
  55.5 1.0 %collective-permute-start.18 = (bf16[64,1024]{1,0:T(8,128)(2,1)S(1)}, bf16[64,1024]{1,0:T(8,128)(2,1)S(1)}, u32[]{:S(2)}, u32[]{:S(2)}) collective-permute-start(bf16[64,1024]{1,0:T(8,128)(2,1)S(1)} %get-tuple-element.46), channel_id=1, source_target_pairs={{0,4},{4,0},{8,12},{12,8},{16,20},{20,16},{24,28},{28,24},{1,5},{5... | collective-permute-start | bytes 393224 | tf_op jit(solution)/shard_map/ppermute | solution.py:584
  56.7 1.1 %collective-permute-start.16 = (bf16[64,1024]{1,0:T(8,128)(2,1)S(1)}, bf16[64,1024]{1,0:T(8,128)(2,1)S(1)}, u32[]{:S(2)}, u32[]{:S(2)}) collective-permute-start(bf16[64,1024]{1,0:T(8,128)(2,1)S(1)} %get-tuple-element.41), channel_id=1, source_target_pairs={{0,4},{4,0},{8,12},{12,8},{16,20},{20,16},{24,28},{28,24},{1,5},{5... | collective-permute-start | bytes 393224 | tf_op jit(solution)/shard_map/ppermute | solution.py:584
  57.7 4.2 %collective-permute-done.18.other = bf16[64,1024]{1,0:T(8,128)(2,1)S(1)} collective-permute-done((bf16[64,1024]{1,0:T(8,128)(2,1)S(1)}, bf16[64,1024]{1,0:T(8,128)(2,1)S(1)}, u32[]{:S(2)}, u32[]{:S(2)}) %collective-permute-start.18) | collective-permute-done | bytes 131104 | tf_op jit(solution)/shard_map/ppermute | solution.py:584
  62.3 2.1 %collective-permute-start.20 = (bf16[32,1024]{1,0:T(8,128)(2,1)S(1)}, bf16[32,1024]{1,0:T(8,128)(2,1)S(1)}, u32[]{:S(2)}, u32[]{:S(2)}) collective-permute-start(bf16[32,1024]{1,0:T(8,128)(2,1)S(1)} %get-tuple-element.48), channel_id=1, source_target_pairs={{0,24},{4,28},{8,16},{12,20},{16,8},{20,12},{24,0},{28,4},{1,25},{... | collective-permute-start | bytes 196616 | tf_op jit(solution)/shard_map/ppermute | solution.py:584
  64.4 1.1 %collective-permute-start.21 = (bf16[32,1024]{1,0:T(8,128)(2,1)S(1)}, bf16[32,1024]{1,0:T(8,128)(2,1)S(1)}, u32[]{:S(2)}, u32[]{:S(2)}) collective-permute-start(bf16[32,1024]{1,0:T(8,128)(2,1)S(1)} %get-tuple-element.49), channel_id=1, source_target_pairs={{0,8},{4,12},{8,0},{12,4},{16,24},{20,28},{24,16},{28,20},{1,9},{5... | collective-permute-start | bytes 196616 | tf_op jit(solution)/shard_map/ppermute | solution.py:584
  65.6 2.1 %collective-permute-done.19.refs_1_ = bf16[32,1024]{1,0:T(8,128)(2,1)S(1)} collective-permute-done((bf16[32,1024]{1,0:T(8,128)(2,1)S(1)}, bf16[32,1024]{1,0:T(8,128)(2,1)S(1)}, u32[]{:S(2)}, u32[]{:S(2)}) %collective-permute-start.19) | collective-permute-done | bytes 65568 | tf_op jit(solution)/shard_map/ppermute | solution.py:584
  69.3 1.5 %collective-permute-start.22 = (f32[8,32]{1,0:T(8,128)S(1)}, f32[8,32]{1,0:T(8,128)S(1)}, u32[]{:S(2)}, u32[]{:S(2)}) collective-permute-start(f32[8,32]{1,0:T(8,128)S(1)} %get-tuple-element.51), channel_id=1, source_target_pairs={{0,1},{1,0},{2,3},{3,2},{4,5},{5,4},{6,7},{7,6},{8,9},{9,8},{10,11... | collective-permute-start | bytes 3080 | tf_op jit(solution)/shard_map/ppermute | solution.py:587
  71.4 1.5 %collective-permute-done.22 = f32[8,32]{1,0:T(8,128)S(1)} collective-permute-done((f32[8,32]{1,0:T(8,128)S(1)}, f32[8,32]{1,0:T(8,128)S(1)}, u32[]{:S(2)}, u32[]{:S(2)}) %collective-permute-start.22) | collective-permute-done | bytes 1056 | tf_op jit(solution)/shard_map/ppermute | solution.py:587
  (60 shorter events, 7.6 us)
Async XLA Ops:
  1.3 12.8 %copy-start.7 = (s32[256]{0:T(256)S(1)}, s32[256]{0:T(256)}, u32[]{:S(2)}) copy-start(s32[256]{0:T(256)} %param.24) | copy-start | bytes 3076
  1.3 13.0 %copy-start.3 = (bf16[32,2048]{1,0:T(8,128)(2,1)S(1)}, bf16[32,2048]{1,0:T(8,128)(2,1)}, u32[]{:S(2)}) copy-start(bf16[32,2048]{1,0:T(8,128)(2,1)} %param.16) | copy-start | bytes 393220
  1.3 14.2 %copy-start.5 = (bf16[1024]{0:T(1024)(128)(2,1)S(1)}, bf16[1024]{0:T(1024)(128)(2,1)}, u32[]{:S(2)}) copy-start(bf16[1024]{0:T(1024)(128)(2,1)} %param.30) | copy-start | bytes 6148
  1.3 14.3 %copy-start.6 = (bf16[1024]{0:T(1024)(128)(2,1)S(1)}, bf16[1024]{0:T(1024)(128)(2,1)}, u32[]{:S(2)}) copy-start(bf16[1024]{0:T(1024)(128)(2,1)} %param.31) | copy-start | bytes 6148
  1.3 14.3 %copy-start.4 = (bf16[2048]{0:T(1024)(128)(2,1)S(1)}, bf16[2048]{0:T(1024)(128)(2,1)}, u32[]{:S(2)}) copy-start(bf16[2048]{0:T(1024)(128)(2,1)} %param.26) | copy-start | bytes 12292
  1.3 31.0 %copy-start = (bf16[1024,384]{1,0:T(8,128)(2,1)S(1)}, bf16[1024,384]{1,0:T(8,128)(2,1)}, u32[]{:S(2)}) copy-start(bf16[1024,384]{1,0:T(8,128)(2,1)} %refs_1_.3) | copy-start | bytes 2359300
  1.3 31.0 %copy-start.1 = (bf16[1024,384]{1,0:T(8,128)(2,1)S(1)}, bf16[1024,384]{1,0:T(8,128)(2,1)}, u32[]{:S(2)}) copy-start(bf16[1024,384]{1,0:T(8,128)(2,1)} %refs_2_.3) | copy-start | bytes 2359300
  11.0 6.2 %collective-permute-start = (bf16[32,2048]{1,0:T(8,128)(2,1)}, bf16[32,2048]{1,0:T(8,128)(2,1)S(1)}, u32[]{:S(2)}, u32[]{:S(2)}) collective-permute-start(bf16[32,2048]{1,0:T(8,128)(2,1)} %get-tuple-element.28), channel_id=1, source_target_pairs={{0,1},{1,0},{2,3},{3,2},{4,5},{5,4},{6,7},{7,6},{8,9},{9,8},{10,11... | collective-permute-start | bytes 393224 | tf_op jit(solution)/shard_map/ppermute | solution.py:587
  17.3 35.6 %copy-start.2 = (bf16[384,1024]{1,0:T(8,128)(2,1)S(1)}, bf16[384,1024]{1,0:T(8,128)(2,1)}, u32[]{:S(2)}) copy-start(bf16[384,1024]{1,0:T(8,128)(2,1)} %refs_6_.3) | copy-start | bytes 2359300
  17.4 7.2 %collective-permute-start.2 = (bf16[32,1024]{1,0:T(8,128)(2,1)S(1)}, bf16[32,1024]{1,0:T(8,128)(2,1)S(1)}, u32[]{:S(2)}, u32[]{:S(2)}) collective-permute-start(bf16[32,1024]{1,0:T(8,128)(2,1)S(1)} %bitcast.11), channel_id=1, source_target_pairs={{0,8},{4,12},{8,0},{12,4},{16,24},{20,28},{24,16},{28,20},{1,9},{5... | collective-permute-start | bytes 196616 | tf_op jit(solution)/shard_map/ppermute | solution.py:584
  22.1 6.2 %collective-permute-start.3 = (bf16[32,1024]{1,0:T(8,128)(2,1)S(1)}, bf16[32,1024]{1,0:T(8,128)(2,1)S(1)}, u32[]{:S(2)}, u32[]{:S(2)}) collective-permute-start(bf16[32,1024]{1,0:T(8,128)(2,1)S(1)} %bitcast.12), channel_id=1, source_target_pairs={{0,24},{4,28},{8,16},{12,20},{16,8},{20,12},{24,0},{28,4},{1,25},{... | collective-permute-start | bytes 196616 | tf_op jit(solution)/shard_map/ppermute | solution.py:584
  22.3 7.8 %collective-permute-start.1 = (bf16[32,1024]{1,0:T(8,128)(2,1)S(1)}, bf16[32,1024]{1,0:T(8,128)(2,1)S(1)}, u32[]{:S(2)}, u32[]{:S(2)}) collective-permute-start(bf16[32,1024]{1,0:T(8,128)(2,1)S(1)} %bitcast.13), channel_id=1, source_target_pairs={{0,16},{4,20},{8,24},{12,28},{16,0},{20,4},{24,8},{28,12},{1,17},{... | collective-permute-start | bytes 196616 | tf_op jit(solution)/shard_map/ppermute | solution.py:584
  28.3 4.0 %collective-permute-start.5 = (bf16[64,1024]{1,0:T(8,128)(2,1)S(1)}, bf16[64,1024]{1,0:T(8,128)(2,1)S(1)}, u32[]{:S(2)}, u32[]{:S(2)}) collective-permute-start(bf16[64,1024]{1,0:T(8,128)(2,1)S(1)} %pack.4.refs_1_), channel_id=1, source_target_pairs={{0,2},{2,0},{1,3},{3,1},{4,6},{6,4},{5,7},{7,5},{8,10},{10,8},{9,1... | collective-permute-start | bytes 393224 | tf_op jit(solution)/shard_map/ppermute | solution.py:587
  30.1 2.2 %collective-permute-start.4 = (bf16[64,1024]{1,0:T(8,128)(2,1)S(1)}, bf16[64,1024]{1,0:T(8,128)(2,1)S(1)}, u32[]{:S(2)}, u32[]{:S(2)}) collective-permute-start(bf16[64,1024]{1,0:T(8,128)(2,1)S(1)} %pack.3.refs_0_), channel_id=1, source_target_pairs={{0,2},{2,0},{1,3},{3,1},{4,6},{6,4},{5,7},{7,5},{8,10},{10,8},{9,1... | collective-permute-start | bytes 393224 | tf_op jit(solution)/shard_map/ppermute | solution.py:587
  30.2 6.4 %collective-permute-start.10 = (bf16[64,1024]{1,0:T(8,128)(2,1)S(1)}, bf16[64,1024]{1,0:T(8,128)(2,1)S(1)}, u32[]{:S(2)}, u32[]{:S(2)}) collective-permute-start(bf16[64,1024]{1,0:T(8,128)(2,1)S(1)} %pack.4.refs_1_), channel_id=1, source_target_pairs={{0,4},{4,0},{8,12},{12,8},{16,20},{20,16},{24,28},{28,24},{1,5},{5... | collective-permute-start | bytes 393224 | tf_op jit(solution)/shard_map/ppermute | solution.py:584
  31.2 7.8 %collective-permute-start.9 = (bf16[64,1024]{1,0:T(8,128)(2,1)S(1)}, bf16[64,1024]{1,0:T(8,128)(2,1)S(1)}, u32[]{:S(2)}, u32[]{:S(2)}) collective-permute-start(bf16[64,1024]{1,0:T(8,128)(2,1)S(1)} %pack.3.refs_0_), channel_id=1, source_target_pairs={{0,4},{4,0},{8,12},{12,8},{16,20},{20,16},{24,28},{28,24},{1,5},{5... | collective-permute-start | bytes 393224 | tf_op jit(solution)/shard_map/ppermute | solution.py:584
  33.1 5.9 %collective-permute-start.6 = (bf16[64,768]{1,0:T(8,128)(2,1)S(1)}, bf16[64,768]{1,0:T(8,128)(2,1)S(1)}, u32[]{:S(2)}, u32[]{:S(2)}) collective-permute-start(bf16[64,768]{1,0:T(8,128)(2,1)S(1)} %get-tuple-element.31), channel_id=1, source_target_pairs={{0,1},{1,0},{2,3},{3,2},{4,5},{5,4},{6,7},{7,6},{8,9},{9,8},{10,11... | collective-permute-start | bytes 294920 | tf_op jit(solution)/shard_map/ppermute | solution.py:587
  34.6 5.2 %collective-permute-start.7 = (bf16[64,768]{1,0:T(8,128)(2,1)S(1)}, bf16[64,768]{1,0:T(8,128)(2,1)S(1)}, u32[]{:S(2)}, u32[]{:S(2)}) collective-permute-start(bf16[64,768]{1,0:T(8,128)(2,1)S(1)} %get-tuple-element.32), channel_id=1, source_target_pairs={{0,1},{1,0},{2,3},{3,2},{4,5},{5,4},{6,7},{7,6},{8,9},{9,8},{10,11... | collective-permute-start | bytes 294920 | tf_op jit(solution)/shard_map/ppermute | solution.py:587
  39.9 2.1 %collective-permute-start.11 = (bf16[128,1024]{1,0:T(8,128)(2,1)S(1)}, bf16[128,1024]{1,0:T(8,128)(2,1)S(1)}, u32[]{:S(2)}, u32[]{:S(2)}) collective-permute-start(bf16[128,1024]{1,0:T(8,128)(2,1)S(1)} %pack.5.refs_0_), channel_id=1, source_target_pairs={{0,2},{2,0},{1,3},{3,1},{4,6},{6,4},{5,7},{7,5},{8,10},{10,8},{9,1... | collective-permute-start | bytes 786440 | tf_op jit(solution)/shard_map/ppermute | solution.py:587
  40.4 5.6 %collective-permute-start.12 = (bf16[64,768]{1,0:T(8,128)(2,1)S(1)}, bf16[64,768]{1,0:T(8,128)(2,1)S(1)}, u32[]{:S(2)}, u32[]{:S(2)}) collective-permute-start(bf16[64,768]{1,0:T(8,128)(2,1)S(1)} %get-tuple-element.35), channel_id=1, source_target_pairs={{0,1},{1,0},{2,3},{3,2},{4,5},{5,4},{6,7},{7,6},{8,9},{9,8},{10,11... | collective-permute-start | bytes 294920 | tf_op jit(solution)/shard_map/ppermute | solution.py:587
  42.4 5.7 %collective-permute-start.13 = (bf16[64,768]{1,0:T(8,128)(2,1)S(1)}, bf16[64,768]{1,0:T(8,128)(2,1)S(1)}, u32[]{:S(2)}, u32[]{:S(2)}) collective-permute-start(bf16[64,768]{1,0:T(8,128)(2,1)S(1)} %get-tuple-element.36), channel_id=1, source_target_pairs={{0,1},{1,0},{2,3},{3,2},{4,5},{5,4},{6,7},{7,6},{8,9},{9,8},{10,11... | collective-permute-start | bytes 294920 | tf_op jit(solution)/shard_map/ppermute | solution.py:587
  43.6 6.3 %collective-permute-start.8 = (bf16[128,384]{1,0:T(8,128)(2,1)S(1)}, bf16[128,384]{1,0:T(8,128)(2,1)S(1)}, u32[]{:S(2)}, u32[]{:S(2)}) collective-permute-start(bf16[128,384]{1,0:T(8,128)(2,1)S(1)} %hidden.2.refs_0_), channel_id=1, source_target_pairs={{0,1},{1,0},{2,3},{3,2},{4,5},{5,4},{6,7},{7,6},{8,9},{9,8},{10,11... | collective-permute-start | bytes 294920 | tf_op jit(solution)/shard_map/ppermute | solution.py:587
  48.2 4.7 %collective-permute-start.14 = (bf16[128,384]{1,0:T(8,128)(2,1)S(1)}, bf16[128,384]{1,0:T(8,128)(2,1)S(1)}, u32[]{:S(2)}, u32[]{:S(2)}) collective-permute-start(bf16[128,384]{1,0:T(8,128)(2,1)S(1)} %hidden.3.refs_2_), channel_id=1, source_target_pairs={{0,1},{1,0},{2,3},{3,2},{4,5},{5,4},{6,7},{7,6},{8,9},{9,8},{10,11... | collective-permute-start | bytes 294920 | tf_op jit(solution)/shard_map/ppermute | solution.py:587
  53.8 1.6 %collective-permute-start.17 = (bf16[128,1024]{1,0:T(8,128)(2,1)S(1)}, bf16[128,1024]{1,0:T(8,128)(2,1)S(1)}, u32[]{:S(2)}, u32[]{:S(2)}) collective-permute-start(bf16[128,1024]{1,0:T(8,128)(2,1)S(1)} %get-tuple-element.44), channel_id=1, source_target_pairs={{0,2},{2,0},{1,3},{3,1},{4,6},{6,4},{5,7},{7,5},{8,10},{10,8},{9,1... | collective-permute-start | bytes 786440 | tf_op jit(solution)/shard_map/ppermute | solution.py:587
  54.9 1.7 %collective-permute-start.15 = (bf16[128,1024]{1,0:T(8,128)(2,1)S(1)}, bf16[128,1024]{1,0:T(8,128)(2,1)S(1)}, u32[]{:S(2)}, u32[]{:S(2)}) collective-permute-start(bf16[128,1024]{1,0:T(8,128)(2,1)S(1)} %get-tuple-element.39), channel_id=1, source_target_pairs={{0,2},{2,0},{1,3},{3,1},{4,6},{6,4},{5,7},{7,5},{8,10},{10,8},{9,1... | collective-permute-start | bytes 786440 | tf_op jit(solution)/shard_map/ppermute | solution.py:587
  55.5 6.4 %collective-permute-start.18 = (bf16[64,1024]{1,0:T(8,128)(2,1)S(1)}, bf16[64,1024]{1,0:T(8,128)(2,1)S(1)}, u32[]{:S(2)}, u32[]{:S(2)}) collective-permute-start(bf16[64,1024]{1,0:T(8,128)(2,1)S(1)} %get-tuple-element.46), channel_id=1, source_target_pairs={{0,4},{4,0},{8,12},{12,8},{16,20},{20,16},{24,28},{28,24},{1,5},{5... | collective-permute-start | bytes 393224 | tf_op jit(solution)/shard_map/ppermute | solution.py:584
  56.7 7.8 %collective-permute-start.16 = (bf16[64,1024]{1,0:T(8,128)(2,1)S(1)}, bf16[64,1024]{1,0:T(8,128)(2,1)S(1)}, u32[]{:S(2)}, u32[]{:S(2)}) collective-permute-start(bf16[64,1024]{1,0:T(8,128)(2,1)S(1)} %get-tuple-element.41), channel_id=1, source_target_pairs={{0,4},{4,0},{8,12},{12,8},{16,20},{20,16},{24,28},{28,24},{1,5},{5... | collective-permute-start | bytes 393224 | tf_op jit(solution)/shard_map/ppermute | solution.py:584
  61.9 5.8 %collective-permute-start.19 = (bf16[32,1024]{1,0:T(8,128)(2,1)S(1)}, bf16[32,1024]{1,0:T(8,128)(2,1)S(1)}, u32[]{:S(2)}, u32[]{:S(2)}) collective-permute-start(bf16[32,1024]{1,0:T(8,128)(2,1)S(1)} %get-tuple-element.47), channel_id=1, source_target_pairs={{0,16},{4,20},{8,24},{12,28},{16,0},{20,4},{24,8},{28,12},{1,17},{... | collective-permute-start | bytes 196616 | tf_op jit(solution)/shard_map/ppermute | solution.py:584
  62.3 6.2 %collective-permute-start.20 = (bf16[32,1024]{1,0:T(8,128)(2,1)S(1)}, bf16[32,1024]{1,0:T(8,128)(2,1)S(1)}, u32[]{:S(2)}, u32[]{:S(2)}) collective-permute-start(bf16[32,1024]{1,0:T(8,128)(2,1)S(1)} %get-tuple-element.48), channel_id=1, source_target_pairs={{0,24},{4,28},{8,16},{12,20},{16,8},{20,12},{24,0},{28,4},{1,25},{... | collective-permute-start | bytes 196616 | tf_op jit(solution)/shard_map/ppermute | solution.py:584
  64.4 4.7 %collective-permute-start.21 = (bf16[32,1024]{1,0:T(8,128)(2,1)S(1)}, bf16[32,1024]{1,0:T(8,128)(2,1)S(1)}, u32[]{:S(2)}, u32[]{:S(2)}) collective-permute-start(bf16[32,1024]{1,0:T(8,128)(2,1)S(1)} %get-tuple-element.49), channel_id=1, source_target_pairs={{0,8},{4,12},{8,0},{12,4},{16,24},{20,28},{24,16},{28,20},{1,9},{5... | collective-permute-start | bytes 196616 | tf_op jit(solution)/shard_map/ppermute | solution.py:584
  69.3 3.6 %collective-permute-start.22 = (f32[8,32]{1,0:T(8,128)S(1)}, f32[8,32]{1,0:T(8,128)S(1)}, u32[]{:S(2)}, u32[]{:S(2)}) collective-permute-start(f32[8,32]{1,0:T(8,128)S(1)} %get-tuple-element.51), channel_id=1, source_target_pairs={{0,1},{1,0},{2,3},{3,2},{4,5},{5,4},{6,7},{7,6},{8,9},{9,8},{10,11... | collective-permute-start | bytes 3080 | tf_op jit(solution)/shard_map/ppermute | solution.py:587
